TPU v7x, 128 devices: a whole 4x4x4 slice. The times are simulated.
128 devices in a mesh: row: 16 (over y_lo, z, core), col: 8 (over x, y_hi).
Axes of the slice: x: 4, y: 4 (y_hi: 2, y_lo: 2; y = y_hi * 2 + y_lo), z: 4, core: 2. Of those that a mesh axis runs over, the one named last changes fastest.
Arguments:
- pair: float32 [1024, 1024, 128], P('row', 'col'), may hold values from -6 to 6
- ln_gain: float32 [128], replicated, may hold values from 0.1 to 1.9
- ln_bias: float32 [128], replicated, may hold values from -3 to 3
- w_left: bfloat16 [128, 256], replicated, may hold values from -0.5 to 0.5
- w_right: bfloat16 [128, 256], replicated, may hold values from -0.5 to 0.5
- w_gate: bfloat16 [128, 128], replicated, may hold values from -0.5 to 0.5
- w_out: bfloat16 [128, 128], replicated, may hold values from -0.5 to 0.5
- out_gain: float32 [128], replicated, may hold values from 0.1 to 1.9
- out_bias: float32 [128], replicated, may hold values from -3 to 3
Outputs:
- update: float32 [1024, 1024, 128], P('row', 'col')
All inputs are finite; a program needn't handle non-finite values.
Results may differ from a plain program's by a relative error of at most 0.018.
Values may be sent and summed in bfloat16 or wider, within the bound.
No kernel may reach another device: no remote copies, remote signals or barrier semaphores. Data moves between devices by JAX's collectives and lax.ppermute only.
A program may use at most 320 MiB of HBM per device.

v0:
```python
import jax
import jax.numpy as jnp
from jax import lax
from jax.sharding import PartitionSpec as P


def layer_norm(values, gain, bias):
    center = jnp.mean(values, axis=-1, keepdims=True)
    spread = jnp.mean((values - center) ** 2, axis=-1, keepdims=True)
    return (values - center) * lax.rsqrt(spread + 1e-05) * gain + bias


def gated_edges(normed, weight):
    half = weight.shape[1] // 2
    projected = jnp.dot(normed, weight, preferred_element_type=jnp.float32)
    return (jax.nn.sigmoid(projected[..., :half]) * projected[..., half:]).astype(jnp.bfloat16)


def per_device(pair, ln_gain, ln_bias, w_left, w_right, w_gate, w_out, out_gain, out_bias):
    normed = layer_norm(pair, ln_gain, ln_bias).astype(jnp.bfloat16)
    left_edges = gated_edges(normed, w_left)
    right_edges = gated_edges(normed, w_right)
    gating = jax.nn.sigmoid(jnp.dot(normed, w_gate, preferred_element_type=jnp.float32))
    gathered = lax.all_gather(left_edges, "col", axis=1, tiled=True)
    product = lax.psum_scatter(
        jnp.einsum(
            "kic,kjc->ijc", gathered, right_edges, preferred_element_type=jnp.float32
        ).astype(jnp.bfloat16),
        "row",
        scatter_dimension=0,
        tiled=True,
    ).astype(jnp.float32)
    product_normed = layer_norm(product, out_gain, out_bias).astype(jnp.bfloat16)
    return gating * jnp.dot(product_normed, w_out, preferred_element_type=jnp.float32)


def solution(mesh):
    return jax.shard_map(
        per_device,
        mesh=mesh,
        in_specs=(P("row", "col", None), P(), P(), P(), P(), P(), P(), P(), P()),
        out_specs=P("row", "col", None),
        check_vma=False,
    )
```

profile of v0, /device:TPU:0, one launch (start us, length us, event | category | flops | bytes accessed | tf_op | source)
XLA Modules:
  0.0 504.3 jit_solution(13013508095744600033)
XLA Ops:
  6.5 0.0 copy-start
  6.5 0.0 copy-start.7
  6.5 0.0 copy-start.6
  6.5 0.0 all-gather.2.cloned.1.call-start
  6.5 3.4 reduce_sum.36
  9.9 0.0 copy-start.2
  10.0 4.1 multiply_reduce_fusion
  14.1 0.0 copy-done.7
  14.1 0.0 copy-done.6
  14.1 0.0 copy-done.2
  14.1 2.5 add_convert_fusion
  16.6 0.0 copy-done
  16.6 1.2 fusion.19
  17.8 0.0 copy-start.4
  17.9 2.4 fusion.6
  20.3 0.0 all-gather.2.cloned.1.call-update
  20.3 0.2 reduce-scatter.2.cloned.1.call-start
  20.6 0.0 copy-done.4
  20.6 1.2 fusion.21
  21.8 2.4 fusion.10
  24.2 4.1 copy.15
  28.4 180.4 %all-gather.2.cloned.1.call-done = bf16[64,1024,128]{2,1,0:T(8,128)(2,1)} async-done(((bf16[64,128,128]{2,1,0:T(8,128)(2,1)}), bf16[64,1024,128]{2,1,0:T(8,128)(2,1)}) %all-gather.2.cloned.1.call-update) | async-done | bytes 16777232 | tf_op jit(solution)/shard_map/all_gather | solution.py:24
  208.8 23.5 %copy.16 = bf16[64,1024,128]{1,0,2:T(8,128)(2,1)} copy(bf16[64,1024,128]{2,1,0:T(8,128)(2,1)} %all-gather.2.cloned.1.call-done) | data formatting | bytes 33554432 | tf_op jit(solution)/shard_map/all_gather | solution.py:24
  232.3 20.7 %convert_bitcast_fusion = bf16[1024,128,128]{0,1,2:T(8,128)(2,1)} fusion(bf16[64,128,128]{1,0,2:T(8,128)(2,1)} %copy.15, bf16[64,1024,128]{1,0,2:T(8,128)(2,1)} %copy.16), kind=kOutput, calls=%fused_computation | convolution fusion | flops 2164260864 | bytes 52428800 | tf_op jit(solution)/shard_map/kic,kjc->ijc/dot_general | solution.py:26
  253.0 51.3 %copy.17 = bf16[1024,128,128]{2,1,0:T(8,128)(2,1)} copy(bf16[1024,128,128]{0,1,2:T(8,128)(2,1)} %convert_bitcast_fusion) | data formatting | bytes 67108864 | tf_op jit(solution)/shard_map/convert_element_type | solution.py:28
  304.3 0.0 copy-start.5
  304.3 0.0 reduce-scatter.2.cloned.1.call-update
  304.4 0.7 copy-done.5
  305.1 0.0 copy-start.8
  305.1 0.0 copy-start.9
  305.1 0.0 copy-start.10
  305.1 2.7 fusion.24
  307.8 177.4 %reduce-scatter.2.cloned.1.call-done = bf16[64,128,128]{2,1,0:T(8,128)(2,1)} async-done(((bf16[1024,128,128]{2,1,0:T(8,128)(2,1)}), bf16[64,128,128]{2,1,0:T(8,128)(2,1)}) %reduce-scatter.2.cloned.1.call-update) | async-done | bytes 2097168 | tf_op jit(solution)/shard_map/reduce_scatter | solution.py:25
  485.2 0.0 copy-start.3
  485.2 2.4 convert_reduce_fusion
  487.6 3.6 fusion.2
  491.2 0.0 copy-done.8
  491.2 0.0 copy-done.9
  491.2 0.0 copy-done.10
  491.2 0.0 copy-done.3
  491.2 0.0 copy-start.1
  491.3 6.2 %divide_multiply_fusion = f32[64,128,128]{2,1,0:T(8,128)} fusion(f32[64,128,128]{2,1,0:T(8,128)} %fusion.24, bf16[64,128,128]{2,1,0:T(8,128)(2,1)S(1)} %copy-done.3, f32[128]{0:T(128)S(1)} %copy-done.9, f32[128]{0:T(128)S(1)} %copy-done.10, f32[64,128]{1,0:T(8,128)S(1)} %add_rsqrt_fusion, f32[64,128]{1,0:T(8,128)S(1)} %broadcast_multiply_fusion, ...), kind=kOutput, calls=%fused_computation.21 | convolution fusion | flops 278921216 | bytes 10585088 | tf_op jit(solution)/shard_map/dot_general | solution.py:34
  497.5 0.0 copy-done.1
  (4 shorter events, 0.0 us)
Async XLA Ops:
  6.5 10.1 %copy-start = (bf16[128,256]{1,0:T(8,128)(2,1)S(1)}, bf16[128,256]{1,0:T(8,128)(2,1)}, u32[]{:S(2)}) copy-start(bf16[128,256]{1,0:T(8,128)(2,1)} %param.12) | copy-start | bytes 196612
  6.5 7.5 %copy-start.7 = (f32[128]{0:T(128)S(1)}, f32[128]{0:T(128)}, u32[]{:S(2)}) copy-start(f32[128]{0:T(128)} %param.10) | copy-start | bytes 1540
  6.5 7.5 %copy-start.6 = (f32[128]{0:T(128)S(1)}, f32[128]{0:T(128)}, u32[]{:S(2)}) copy-start(f32[128]{0:T(128)} %param.11) | copy-start | bytes 1540
  6.5 202.3 %all-gather.2.cloned.1.call-start = ((), (), s32[]{:S(2)}) async-start(), calls=%async_computation.1 | async-start | bytes 18874368 | tf_op jit(solution)/shard_map/all_gather | solution.py:24
  9.9 4.2 copy-start.2
  17.8 2.7 copy-start.4
  20.3 464.9 %reduce-scatter.2.cloned.1.call-start = ((), (), s32[]{:S(2)}) async-start(), calls=%async_computation.2 | async-start | bytes 35651584 | tf_op jit(solution)/shard_map/reduce_scatter | solution.py:25
  304.3 0.8 copy-start.5
  305.1 186.1 %copy-start.8 = (bf16[128,128]{1,0:T(8,128)(2,1)S(1)}, bf16[128,128]{1,0:T(8,128)(2,1)}, u32[]{:S(2)}) copy-start(bf16[128,128]{1,0:T(8,128)(2,1)} %param.15) | copy-start | bytes 98308
  305.1 186.1 %copy-start.9 = (f32[128]{0:T(128)S(1)}, f32[128]{0:T(128)}, u32[]{:S(2)}) copy-start(f32[128]{0:T(128)} %param.17) | copy-start | bytes 1540
  305.1 186.1 %copy-start.10 = (f32[128]{0:T(128)S(1)}, f32[128]{0:T(128)}, u32[]{:S(2)}) copy-start(f32[128]{0:T(128)} %param.16) | copy-start | bytes 1540
  485.2 6.0 %copy-start.3 = (bf16[64,128,128]{2,1,0:T(8,128)(2,1)S(1)}, bf16[64,128,128]{2,1,0:T(8,128)(2,1)}, u32[]{:S(2)}) copy-start(bf16[64,128,128]{2,1,0:T(8,128)(2,1)} %reduce-scatter.2.cloned.1.call-done) | copy-start | bytes 6291460
  491.2 6.2 %copy-start.1 = (bf16[128,256]{1,0:T(8,128)(2,1)S(1)}, bf16[128,256]{1,0:T(8,128)(2,1)}, u32[]{:S(2)}) copy-start(bf16[128,256]{1,0:T(8,128)(2,1)} %param.12) | copy-start | bytes 196612
Sparse Core Ops, SparseCore 0:
  20.5 188.3 all-gather.1
  304.5 180.6 reduce-scatter.1
where the time goes:
time: 506 us; the launch traced here: 504 us
  waiting for transfers between devices  358 us (71%)
  local copies, waits for them, and re-layouts  79.7 us (16%)
  matrix products  32.1 us (6%)
  other arithmetic  20.8 us (4%)
  between operations  13.6 us (3%)
    all_gather x1, waiting for transfers between devices, per_device(): gathered = lax.all_gather(left_edges, 'col', axis=1, tiled=True)  180 us
    reduce_scatter x1, waiting for transfers between devices, per_device(): lax.psum_scatter(jnp.einsum('kic,kjc->ijc', gathered, right_edges, prefer...  177 us
    convert_element_type x1, local copies, waits for them, and re-layouts, per_device(): product = lax.psum_scatter(jnp.einsum('kic,kjc->ijc', gathered, right_edg...  51.3 us
    all_gather x1, local copies, waits for them, and re-layouts, per_device(): gathered = lax.all_gather(left_edges, 'col', axis=1, tiled=True)  23.5 us
    dot_general x1, matrix products, per_device(): jnp.einsum('kic,kjc->ijc', gathered, right_edges, preferred_element_type=...  20.7 us
  transfers between devices with their start and end apart: 2, of which 2 were waited for; matrix products, arithmetic and copies ran while one was open for 2% of the time, Pallas kernels for 0%

commit v1 on v0

v1 whole, which is shorter than its diff:
```python
import jax
import jax.numpy as jnp
from jax import lax
from jax.experimental import pallas as pl
from jax.experimental.pallas import tpu as pltpu
from jax.sharding import PartitionSpec as P

F32, BF16 = jnp.float32, jnp.bfloat16
EPS = 1e-05
ROWS = 16
VMEM = 48 * 2**20


def sigmoid(values):
    return 0.5 * jnp.tanh(0.5 * values) + 0.5


def normalize(values, gain, bias):
    center = jnp.mean(values, axis=-1, keepdims=True)
    values = values - center
    spread = jnp.mean(values * values, axis=-1, keepdims=True)
    return (values * lax.rsqrt(spread + EPS) * gain + bias).astype(BF16)


def edges_kernel(pair, gain, bias, weight, left, right, left_rows, right_rows):
    rows, tokens, channels = pair.shape
    for row in range(0, rows, 2):
        normed = normalize(pair[row : row + 2].reshape(2 * tokens, channels), gain[...], bias[...])
        projected = lax.dot_general(
            weight[...], normed, (((1,), (1,)), ((), ())), preferred_element_type=F32
        )
        lefts = sigmoid(projected[:channels]) * projected[channels : 2 * channels]
        rights = sigmoid(projected[2 * channels : 3 * channels]) * projected[3 * channels :]
        for half in range(2):
            place = pl.ds((row + half) * channels, channels)
            lanes = slice(half * tokens, (half + 1) * tokens)
            left_rows[place, :] = lefts[:, lanes]
            right_rows[place, :] = rights[:, lanes]
    for channel in range(channels):
        left[channel] = left_rows[pl.ds(channel, rows, stride=channels), :].astype(BF16)
        right[channel] = right_rows[pl.ds(channel, rows, stride=channels), :].astype(BF16)


def edges(pair, gain, bias, weight):
    rows, tokens, channels = pair.shape
    whole = lambda *shape: pl.BlockSpec(shape, lambda step: (0,) * len(shape))
    out = pl.BlockSpec((channels, ROWS, tokens), lambda step: (0, step, 0))
    return pl.pallas_call(
        edges_kernel,
        grid=(rows // ROWS,),
        in_specs=[
            pl.BlockSpec((ROWS, tokens, channels), lambda step: (step, 0, 0)),
            whole(1, channels),
            whole(1, channels),
            whole(4 * channels, channels),
        ],
        out_specs=[out, out],
        out_shape=[jax.ShapeDtypeStruct((channels, rows, tokens), BF16)] * 2,
        scratch_shapes=[pltpu.VMEM((ROWS * channels, tokens), F32)] * 2,
        compiler_params=pltpu.CompilerParams(vmem_limit_bytes=VMEM),
        cost_estimate=pl.CostEstimate(
            flops=8 * rows * tokens * channels * channels,
            bytes_accessed=8 * rows * tokens * channels,
            transcendentals=2 * rows * tokens * channels,
        ),
        name="edges",
    )(pair, gain, bias, weight)


def gating_kernel(pair, gain, bias, weight, gating):
    rows, tokens, channels = pair.shape
    normed = normalize(pair[...].reshape(rows * tokens, channels), gain[...], bias[...])
    projected = jnp.dot(normed, weight[...], preferred_element_type=F32)
    gating[...] = sigmoid(projected).reshape(rows, tokens, channels)


def gates(pair, gain, bias, weight):
    rows, tokens, channels = pair.shape
    whole = lambda *shape: pl.BlockSpec(shape, lambda step: (0,) * len(shape))
    block = pl.BlockSpec((ROWS, tokens, channels), lambda step: (step, 0, 0))
    return pl.pallas_call(
        gating_kernel,
        grid=(rows // ROWS,),
        in_specs=[block, whole(1, channels), whole(1, channels), whole(channels, channels)],
        out_specs=block,
        out_shape=jax.ShapeDtypeStruct(pair.shape, F32),
        compiler_params=pltpu.CompilerParams(vmem_limit_bytes=VMEM),
        cost_estimate=pl.CostEstimate(
            flops=2 * rows * tokens * channels * channels,
            bytes_accessed=8 * rows * tokens * channels,
            transcendentals=rows * tokens * channels,
        ),
        name="gates",
    )(pair, gain, bias, weight)


def product_kernel(left, right, out, left_turned, right_whole):
    n_rows, n_cols, depth, tokens = left.shape
    for col in range(n_cols):
        lanes = slice(col * tokens, (col + 1) * tokens)
        for row in range(n_rows):
            right_whole[row * depth : (row + 1) * depth, lanes] = right[row, col]
        column = jnp.concatenate([left[row, col] for row in range(n_rows)], axis=0)
        left_turned[lanes, :] = column.T
    wide = 2 * tokens
    for start in range(0, n_cols * tokens, wide):
        total = jnp.dot(
            left_turned[...], right_whole[:, start : start + wide], preferred_element_type=F32
        ).astype(BF16)
        for part in range(2):
            block = total[:, part * tokens : (part + 1) * tokens]
            out[:, start // tokens + part] = block.reshape(n_rows, depth, tokens)


def products(left, right):
    n_rows, n_cols, depth, tokens = left.shape
    size = n_rows * depth
    return pl.pallas_call(
        product_kernel,
        out_shape=jax.ShapeDtypeStruct(left.shape, BF16),
        scratch_shapes=[pltpu.VMEM((size, size), BF16)] * 2,
        compiler_params=pltpu.CompilerParams(vmem_limit_bytes=VMEM),
        cost_estimate=pl.CostEstimate(
            flops=2 * size**3, bytes_accessed=6 * size * size, transcendentals=0
        ),
        name="products",
    )(left, right)


def update_kernel(product, gating, gain, bias, weight, out, rows_of):
    channels, rows, tokens = product.shape
    values = product[...].astype(F32)
    center = jnp.sum(values, axis=0, keepdims=True) * (1.0 / channels)
    values = values - center
    spread = jnp.sum(values * values, axis=0, keepdims=True) * (1.0 / channels)
    values = values * lax.rsqrt(spread + EPS) * gain[...] + bias[...]
    rows_of[...] = values.reshape(channels * rows, tokens)
    for row in range(rows):
        normed = rows_of[pl.ds(row, channels, stride=rows), :].astype(BF16)
        projected = lax.dot_general(
            normed, weight[...], (((0,), (0,)), ((), ())), preferred_element_type=F32
        )
        out[row] = gating[row] * projected


def update(product, gating, gain, bias, weight):
    channels, rows, tokens = product.shape
    whole = lambda *shape: pl.BlockSpec(shape, lambda step: (0,) * len(shape))
    block = pl.BlockSpec((ROWS, tokens, channels), lambda step: (step, 0, 0))
    spread = lambda vector: jnp.broadcast_to(vector[:, None, None], (channels, 1, tokens))
    return pl.pallas_call(
        update_kernel,
        grid=(rows // ROWS,),
        in_specs=[
            pl.BlockSpec((channels, ROWS, tokens), lambda step: (0, step, 0)),
            block,
            whole(channels, 1, tokens),
            whole(channels, 1, tokens),
            whole(channels, channels),
        ],
        out_specs=block,
        out_shape=jax.ShapeDtypeStruct((rows, tokens, channels), F32),
        scratch_shapes=[pltpu.VMEM((channels * ROWS, tokens), F32)],
        compiler_params=pltpu.CompilerParams(vmem_limit_bytes=VMEM),
        cost_estimate=pl.CostEstimate(
            flops=2 * rows * tokens * channels * channels,
            bytes_accessed=10 * rows * tokens * channels,
            transcendentals=0,
        ),
        name="update",
    )(product, gating, spread(gain), spread(bias), weight)


def per_device(n_rows, n_cols, pair, ln_gain, ln_bias, w_left, w_right, w_gate, w_out, out_gain, out_bias):
    rows, tokens, channels = pair.shape
    axes = ("row", "col")
    gain, bias = ln_gain[None], ln_bias[None]
    weight = jnp.concatenate([w_left.T, w_right.T], axis=0)
    left, right = edges(pair, gain, bias, weight)
    gating = gates(pair, gain, bias, w_gate)
    grid = (n_rows, n_cols, rows, tokens)
    left = lax.all_to_all(left, axes, 0, 0, tiled=True).reshape(grid)
    right = lax.all_to_all(right, axes, 0, 0, tiled=True).reshape(grid)
    product = products(left, right).reshape(channels, rows, tokens)
    product = lax.all_to_all(product, axes, 0, 0, tiled=True)
    return update(product, gating, out_gain, out_bias, w_out)


def solution(mesh):
    n_rows, n_cols = mesh.shape["row"], mesh.shape["col"]
    return jax.shard_map(
        lambda *args: per_device(n_rows, n_cols, *args),
        mesh=mesh,
        in_specs=(P("row", "col", None), P(), P(), P(), P(), P(), P(), P(), P()),
        out_specs=P("row", "col", None),
        check_vma=False,
    )
```

time: 506 us -> 138 us (0.27)
  waiting for transfers between devices: 358 us -> 22.4 us
  blocking collectives: 0 us -> 74.5 us
  local copies, waits for them, and re-layouts: 79.7 us -> 6.87 us
  matrix products: 32.1 us -> 0 us
  Pallas kernels: 0 us -> 28.3 us
  other arithmetic: 20.8 us -> 0.01 us
  between operations: 13.6 us -> 0.16 us
    all_gather x1 -> x0, waiting for transfers between devices: 180 us -> none  [per_device(): gathered = lax.all_gather(left_edges, 'col', axis=1, tiled=True)]
    reduce_scatter x1 -> x0, waiting for transfers between devices: 177 us -> none  [per_device(): lax.psum_scatter(jnp.einsum('kic,kjc->ijc', gathered, right_edges, prefer...]
    all_to_all x0 -> x2, blocking collectives: none -> 74.5 us  [the longest x1 40.4 us: per_device(): left = lax.all_to_all(left, axes, 0, 0, tiled=True).reshape(grid)]
    convert_element_type x2 -> x0, local copies, waits for them, and re-layouts: 55.5 us -> none  [the longest x1 51.3 us: per_device(): product = lax.psum_scatter(jnp.einsum('kic,kjc->ijc', gathered, right_edg...]
    dot_general x5 -> x0, matrix products: 32.1 us -> none  [the longest x1 20.7 us: per_device(): jnp.einsum('kic,kjc->ijc', gathered, right_edges, preferred_element_type=...]
    pallas_call x0 -> x4, Pallas kernels: none -> 28.3 us  [the longest x1 11.9 us: edges(): pl.pallas_call(edges_kernel, grid=(rows // ROWS,), in_specs=[pl.BlockSpec...]
    all_gather x1 -> x0, local copies, waits for them, and re-layouts: 23.5 us -> none  [per_device(): gathered = lax.all_gather(left_edges, 'col', axis=1, tiled=True)]
    all_to_all x0 -> x1, waiting for transfers between devices: none -> 22.4 us  [per_device(): product = lax.all_to_all(product, axes, 0, 0, tiled=True)]
  transfers between devices with their start and end apart: 2 -> 1, of which waited for: 2 -> 1; matrix products, arithmetic and copies ran while one was open for 2% -> 0% of each run, Pallas kernels for 0% -> 4%
where the time goes in v1:
time: 138 us; the launch traced here: 137 us
  blocking collectives  74.5 us (54%)
  Pallas kernels  28.3 us (21%)
  waiting for transfers between devices  22.4 us (16%)
  local copies, waits for them, and re-layouts  6.87 us (5%)
  starting transfers between devices  4.83 us (4%)
    all_to_all x1, blocking collectives, per_device(): left = lax.all_to_all(left, axes, 0, 0, tiled=True).reshape(grid)  40.4 us
    all_to_all x1, blocking collectives, per_device(): right = lax.all_to_all(right, axes, 0, 0, tiled=True).reshape(grid)  34.2 us
    all_to_all x1, waiting for transfers between devices, per_device(): product = lax.all_to_all(product, axes, 0, 0, tiled=True)  22.4 us
    pallas_call x1, Pallas kernels, edges(): pl.pallas_call(edges_kernel, grid=(rows // ROWS,), in_specs=[pl.BlockSpec...  11.9 us
    pallas_call x1, Pallas kernels, update(): pl.pallas_call(update_kernel, grid=(rows // ROWS,), in_specs=[pl.BlockSpe...  7.24 us
    unnamed x22, local copies, waits for them, and re-layouts  6.5 us
    pallas_call x1, Pallas kernels, gates(): pl.pallas_call(gating_kernel, grid=(rows // ROWS,), in_specs=[block, whol...  4.99 us
    all_to_all x1, starting transfers between devices, per_device(): product = lax.all_to_all(product, axes, 0, 0, tiled=True)  4.83 us
  transfers between devices with their start and end apart: 1, of which 1 were waited for; matrix products, arithmetic and copies ran while one was open for 0% of the time, Pallas kernels for 4%

profile of v1, /device:TPU:0, one launch (start us, length us, event | category | flops | bytes accessed | tf_op | source)
XLA Modules:
  0.0 137.1 jit_solution(11559581254636106479)
XLA Ops:
  0.0 0.9 copy.10
  1.0 1.0 copy.11
  1.9 0.0 copy-start.4
  1.9 0.6 copy-done.4
  2.6 0.0 copy-start.6
  2.6 0.7 copy-done.6
  3.2 11.9 %edges.1 = (bf16[128,64,128]{2,1,0:T(8,128)(2,1)S(1)}, bf16[128,64,128]{2,1,0:T(8,128)(2,1)S(1)}) custom-call(f32[64,128,128]{2,1,0:T(8,128)} %pair.3, f32[1,128]{1,0:T(1,128)S(1)} %bitcast.9, f32[1,128]{1,0:T(1,128)S(1)} %bitcast.11, bf16[512,128]{1,0:T(8,128)(2,1)S(1)} %pad_maximum_fusion.weight), custom_call_target="tpu_custom_call" | custom-call | flops 1073741824 | bytes 8388608 | tf_op jit(solution)/shard_map/edges/pallas_call | solution.py:48
  15.1 40.4 %all_to_all.15 = bf16[128,64,128]{2,1,0:T(8,128)(2,1)S(1)} all-to-all(bf16[128,64,128]{2,1,0:T(8,128)(2,1)S(1)} %get-tuple-element.7), channel_id=1, replica_groups=mesh['row'=16,'col'=8] {'row','col'}, dimensions={0} | all-to-all | bytes 4194304 | tf_op jit(solution)/shard_map/all_to_all | solution.py:182
  55.5 34.2 %all_to_all.16 = bf16[128,64,128]{2,1,0:T(8,128)(2,1)} all-to-all(bf16[128,64,128]{2,1,0:T(8,128)(2,1)S(1)} %get-tuple-element.8), channel_id=1, replica_groups=mesh['row'=16,'col'=8] {'row','col'}, dimensions={0} | all-to-all | bytes 4194304 | tf_op jit(solution)/shard_map/all_to_all | solution.py:183
  89.7 4.2 %products.1 = bf16[16,8,64,128]{3,2,1,0:T(8,128)(2,1)S(1)} custom-call(bf16[16,8,64,128]{3,2,1,0:T(8,128)(2,1)S(1)} %bitcast.8, bf16[16,8,64,128]{3,2,1,0:T(8,128)(2,1)} %bitcast.13), custom_call_target="tpu_custom_call" | custom-call | flops 2147483648 | bytes 6291456 | tf_op jit(solution)/shard_map/products/pallas_call | solution.py:118
  93.9 0.0 copy-start.1
  93.9 1.3 copy-done.1
  95.2 0.0 copy-start.2
  95.2 0.0 copy-start.5
  95.2 0.0 copy-start.7
  95.2 4.8 %all-to-all-start.2 = ((bf16[128,64,128]{2,1,0:T(8,128)(2,1)}), bf16[128,64,128]{2,1,0:T(8,128)(2,1)S(1)}, u32[]{:S(2)}, u32[]{:S(2)}) async-start(bf16[128,64,128]{2,1,0:T(8,128)(2,1)} %bitcast.7), calls=%async_computation.2 | async-start | bytes 4194304 | tf_op jit(solution)/shard_map/all_to_all | solution.py:185
  100.0 0.0 copy-done.2
  100.0 0.0 copy-done.5
  100.1 0.0 copy-done.7
  100.1 0.0 copy-start.8
  100.1 0.0 copy-start.9
  100.1 0.0 copy-start.3
  100.1 5.0 %gates.1.gating = f32[64,128,128]{2,1,0:T(8,128)S(1)} custom-call(f32[64,128,128]{2,1,0:T(8,128)} %pair.3, f32[1,128]{1,0:T(1,128)S(1)} %bitcast.10, f32[1,128]{1,0:T(1,128)S(1)} %bitcast.12, bf16[128,128]{1,0:T(8,128)(2,1)S(1)} %copy-done.2), custom_call_target="tpu_custom_call" | custom-call | flops 268435456 | bytes 8388608 | tf_op jit(solution)/shard_map/gates/pallas_call | solution.py:81
  105.1 0.0 copy-start
  105.1 1.9 %copy-done = f32[64,128,128]{2,1,0:T(8,128)} copy-done((f32[64,128,128]{2,1,0:T(8,128)}, f32[64,128,128]{2,1,0:T(8,128)S(1)}, u32[]{:S(2)}) %copy-start) | copy-done | bytes 4194328
  107.1 22.4 %all-to-all-done.2.product = bf16[128,64,128]{2,1,0:T(8,128)(2,1)S(1)} async-done(((bf16[128,64,128]{2,1,0:T(8,128)(2,1)}), bf16[128,64,128]{2,1,0:T(8,128)(2,1)S(1)}, u32[]{:S(2)}, u32[]{:S(2)}) %all-to-all-start.2) | async-done | bytes 2097184 | tf_op jit(solution)/shard_map/all_to_all | solution.py:185
  129.5 0.0 copy-done.8
  129.5 0.2 broadcast_in_dim.20.gain
  129.7 0.0 copy-done.9
  129.7 0.2 broadcast_in_dim.21.bias
  129.9 0.0 copy-done.3
  129.9 7.2 %update.1 = f32[64,128,128]{2,1,0:T(8,128)} custom-call(bf16[128,64,128]{2,1,0:T(8,128)(2,1)S(1)} %all-to-all-done.2.product, f32[64,128,128]{2,1,0:T(8,128)} %copy-done, f32[128,1,128]{2,1,0:T(1,128)S(1)} %broadcast_in_dim.20.gain, f32[128,1,128]{2,1,0:T(1,128)S(1)} %broadcast_in_dim.21.bias, bf16[128,128]{1,0:T(8,128)(2,1)S(1)} %copy-done.3), custom_call_target="tpu_custom_call" | custom-call | flops 268435456 | bytes 10485760 | tf_op jit(solution)/shard_map/update/pallas_call | solution.py:151
  (1 shorter events, 0.0 us)
Async XLA Ops:
  1.9 0.7 copy-start.4
  2.6 0.7 copy-start.6
  93.9 1.3 copy-start.1
  95.2 4.8 %copy-start.2 = (bf16[128,128]{1,0:T(8,128)(2,1)S(1)}, bf16[128,128]{1,0:T(8,128)(2,1)}, u32[]{:S(2)}) copy-start(bf16[128,128]{1,0:T(8,128)(2,1)} %weight.2) | copy-start | bytes 98308
  95.2 4.9 %copy-start.5 = (f32[128]{0:T(128)S(1)}, f32[128]{0:T(128)}, u32[]{:S(2)}) copy-start(f32[128]{0:T(128)} %param.10) | copy-start | bytes 1540
  95.2 4.9 %copy-start.7 = (f32[128]{0:T(128)S(1)}, f32[128]{0:T(128)}, u32[]{:S(2)}) copy-start(f32[128]{0:T(128)} %param.11) | copy-start | bytes 1540
  95.2 34.3 %all-to-all-start.2 = ((bf16[128,64,128]{2,1,0:T(8,128)(2,1)}), bf16[128,64,128]{2,1,0:T(8,128)(2,1)S(1)}, u32[]{:S(2)}, u32[]{:S(2)}) async-start(bf16[128,64,128]{2,1,0:T(8,128)(2,1)} %bitcast.7), calls=%async_computation.2 | async-start | bytes 4194304 | tf_op jit(solution)/shard_map/all_to_all | solution.py:185
  100.1 29.4 %copy-start.8 = (f32[128]{0:T(128)S(1)}, f32[128]{0:T(128)}, u32[]{:S(2)}) copy-start(f32[128]{0:T(128)} %param.16) | copy-start | bytes 1540
  100.1 29.6 %copy-start.9 = (f32[128]{0:T(128)S(1)}, f32[128]{0:T(128)}, u32[]{:S(2)}) copy-start(f32[128]{0:T(128)} %param.17) | copy-start | bytes 1540
  100.1 29.8 %copy-start.3 = (bf16[128,128]{1,0:T(8,128)(2,1)S(1)}, bf16[128,128]{1,0:T(8,128)(2,1)}, u32[]{:S(2)}) copy-start(bf16[128,128]{1,0:T(8,128)(2,1)} %weight.3) | copy-start | bytes 98308
  105.1 2.0 %copy-start = (f32[64,128,128]{2,1,0:T(8,128)}, f32[64,128,128]{2,1,0:T(8,128)S(1)}, u32[]{:S(2)}) copy-start(f32[64,128,128]{2,1,0:T(8,128)S(1)} %gates.1.gating) | copy-start | bytes 12582916

commit v2 on v1

--- a/solution.py
+++ b/solution.py
@@ -8,7 +8,7 @@
 F32, BF16 = jnp.float32, jnp.bfloat16
 EPS = 1e-05
 ROWS = 16
-VMEM = 48 * 2**20
+PAD = 4
 
 
 def sigmoid(values):
@@ -22,8 +22,15 @@
     return (values * lax.rsqrt(spread + EPS) * gain + bias).astype(BF16)
 
 
-def edges_kernel(pair, gain, bias, weight, left, right, left_rows, right_rows):
-    rows, tokens, channels = pair.shape
+def edges_kernel(pair, gain, bias, w_left, w_right, out, weight, left_rows, right_rows):
+    rows, tokens, channels = pair.shape
+    pitch = channels + PAD
+
+    @pl.when(pl.program_id(0) == 0)
+    def _():
+        weight[: 2 * channels] = w_left[...].T
+        weight[2 * channels :] = w_right[...].T
+
     for row in range(0, rows, 2):
         normed = normalize(pair[row : row + 2].reshape(2 * tokens, channels), gain[...], bias[...])
         projected = lax.dot_general(
@@ -32,19 +39,19 @@
         lefts = sigmoid(projected[:channels]) * projected[channels : 2 * channels]
         rights = sigmoid(projected[2 * channels : 3 * channels]) * projected[3 * channels :]
         for half in range(2):
-            place = pl.ds((row + half) * channels, channels)
+            place = pl.ds((row + half) * pitch, channels)
             lanes = slice(half * tokens, (half + 1) * tokens)
             left_rows[place, :] = lefts[:, lanes]
             right_rows[place, :] = rights[:, lanes]
     for channel in range(channels):
-        left[channel] = left_rows[pl.ds(channel, rows, stride=channels), :].astype(BF16)
-        right[channel] = right_rows[pl.ds(channel, rows, stride=channels), :].astype(BF16)
-
-
-def edges(pair, gain, bias, weight):
+        place = pl.ds(channel, rows, stride=pitch)
+        out[channel, 0] = left_rows[place, :].astype(BF16)
+        out[channel, 1] = right_rows[place, :].astype(BF16)
+
+
+def edges(pair, gain, bias, w_left, w_right):
     rows, tokens, channels = pair.shape
     whole = lambda *shape: pl.BlockSpec(shape, lambda step: (0,) * len(shape))
-    out = pl.BlockSpec((channels, ROWS, tokens), lambda step: (0, step, 0))
     return pl.pallas_call(
         edges_kernel,
         grid=(rows // ROWS,),
@@ -52,19 +59,21 @@
             pl.BlockSpec((ROWS, tokens, channels), lambda step: (step, 0, 0)),
             whole(1, channels),
             whole(1, channels),
-            whole(4 * channels, channels),
+            whole(channels, 2 * channels),
+            whole(channels, 2 * channels),
         ],
-        out_specs=[out, out],
-        out_shape=[jax.ShapeDtypeStruct((channels, rows, tokens), BF16)] * 2,
-        scratch_shapes=[pltpu.VMEM((ROWS * channels, tokens), F32)] * 2,
-        compiler_params=pltpu.CompilerParams(vmem_limit_bytes=VMEM),
+        out_specs=pl.BlockSpec((channels, 2, ROWS, tokens), lambda step: (0, 0, step, 0)),
+        out_shape=jax.ShapeDtypeStruct((channels, 2, rows, tokens), BF16),
+        scratch_shapes=[pltpu.VMEM((4 * channels, channels), BF16)]
+        + [pltpu.VMEM((ROWS * (channels + PAD), tokens), F32)] * 2,
+        compiler_params=pltpu.CompilerParams(vmem_limit_bytes=16 * 2**20),
         cost_estimate=pl.CostEstimate(
             flops=8 * rows * tokens * channels * channels,
             bytes_accessed=8 * rows * tokens * channels,
             transcendentals=2 * rows * tokens * channels,
         ),
         name="edges",
-    )(pair, gain, bias, weight)
+    )(pair, gain, bias, w_left, w_right)
 
 
 def gating_kernel(pair, gain, bias, weight, gating):
@@ -84,7 +93,7 @@
         in_specs=[block, whole(1, channels), whole(1, channels), whole(channels, channels)],
         out_specs=block,
         out_shape=jax.ShapeDtypeStruct(pair.shape, F32),
-        compiler_params=pltpu.CompilerParams(vmem_limit_bytes=VMEM),
+        compiler_params=pltpu.CompilerParams(vmem_limit_bytes=16 * 2**20),
         cost_estimate=pl.CostEstimate(
             flops=2 * rows * tokens * channels * channels,
             bytes_accessed=8 * rows * tokens * channels,
@@ -94,13 +103,13 @@
     )(pair, gain, bias, weight)
 
 
-def product_kernel(left, right, out, left_turned, right_whole):
-    n_rows, n_cols, depth, tokens = left.shape
+def product_kernel(both, out, left_turned, right_whole):
+    n_rows, n_cols, _, depth, tokens = both.shape
     for col in range(n_cols):
         lanes = slice(col * tokens, (col + 1) * tokens)
         for row in range(n_rows):
-            right_whole[row * depth : (row + 1) * depth, lanes] = right[row, col]
-        column = jnp.concatenate([left[row, col] for row in range(n_rows)], axis=0)
+            right_whole[row * depth : (row + 1) * depth, lanes] = both[row, col, 1]
+        column = jnp.concatenate([both[row, col, 0] for row in range(n_rows)], axis=0)
         left_turned[lanes, :] = column.T
     wide = 2 * tokens
     for start in range(0, n_cols * tokens, wide):
@@ -112,19 +121,19 @@
             out[:, start // tokens + part] = block.reshape(n_rows, depth, tokens)
 
 
-def products(left, right):
-    n_rows, n_cols, depth, tokens = left.shape
+def products(both):
+    n_rows, n_cols, _, depth, tokens = both.shape
     size = n_rows * depth
     return pl.pallas_call(
         product_kernel,
-        out_shape=jax.ShapeDtypeStruct(left.shape, BF16),
+        out_shape=jax.ShapeDtypeStruct((n_rows, n_cols, depth, tokens), BF16),
         scratch_shapes=[pltpu.VMEM((size, size), BF16)] * 2,
-        compiler_params=pltpu.CompilerParams(vmem_limit_bytes=VMEM),
+        compiler_params=pltpu.CompilerParams(vmem_limit_bytes=24 * 2**20),
         cost_estimate=pl.CostEstimate(
             flops=2 * size**3, bytes_accessed=6 * size * size, transcendentals=0
         ),
         name="products",
-    )(left, right)
+    )(both)
 
 
 def update_kernel(product, gating, gain, bias, weight, out, rows_of):
@@ -134,9 +143,11 @@
     values = values - center
     spread = jnp.sum(values * values, axis=0, keepdims=True) * (1.0 / channels)
     values = values * lax.rsqrt(spread + EPS) * gain[...] + bias[...]
-    rows_of[...] = values.reshape(channels * rows, tokens)
+    pitch = rows + PAD
+    for channel in range(channels):
+        rows_of[pl.ds(channel * pitch, rows), :] = values[channel]
     for row in range(rows):
-        normed = rows_of[pl.ds(row, channels, stride=rows), :].astype(BF16)
+        normed = rows_of[pl.ds(row, channels, stride=pitch), :].astype(BF16)
         projected = lax.dot_general(
             normed, weight[...], (((0,), (0,)), ((), ())), preferred_element_type=F32
         )
@@ -160,8 +171,8 @@
         ],
         out_specs=block,
         out_shape=jax.ShapeDtypeStruct((rows, tokens, channels), F32),
-        scratch_shapes=[pltpu.VMEM((channels * ROWS, tokens), F32)],
-        compiler_params=pltpu.CompilerParams(vmem_limit_bytes=VMEM),
+        scratch_shapes=[pltpu.VMEM((channels * (ROWS + PAD), tokens), F32)],
+        compiler_params=pltpu.CompilerParams(vmem_limit_bytes=16 * 2**20),
         cost_estimate=pl.CostEstimate(
             flops=2 * rows * tokens * channels * channels,
             bytes_accessed=10 * rows * tokens * channels,
@@ -175,13 +186,10 @@
     rows, tokens, channels = pair.shape
     axes = ("row", "col")
     gain, bias = ln_gain[None], ln_bias[None]
-    weight = jnp.concatenate([w_left.T, w_right.T], axis=0)
-    left, right = edges(pair, gain, bias, weight)
+    both = edges(pair, gain, bias, w_left, w_right).reshape(channels, 2 * rows, tokens)
     gating = gates(pair, gain, bias, w_gate)
-    grid = (n_rows, n_cols, rows, tokens)
-    left = lax.all_to_all(left, axes, 0, 0, tiled=True).reshape(grid)
-    right = lax.all_to_all(right, axes, 0, 0, tiled=True).reshape(grid)
-    product = products(left, right).reshape(channels, rows, tokens)
+    both = lax.all_to_all(both, axes, 0, 0, tiled=True)
+    product = products(both.reshape(n_rows, n_cols, 2, rows, tokens)).reshape(channels, rows, tokens)
     product = lax.all_to_all(product, axes, 0, 0, tiled=True)
     return update(product, gating, out_gain, out_bias, w_out)
 

time: 138 us -> 120 us (0.87)
  Pallas kernels: 28.3 us -> 15.8 us
  blocking collectives: 74.5 us -> 63.1 us
  local copies, waits for them, and re-layouts: 6.87 us -> 13.3 us
    all_to_all x2 -> x1, blocking collectives: 74.5 us -> 63.1 us  [per_device(): both = lax.all_to_all(both, axes, 0, 0, tiled=True)]
    pallas_call x1, Pallas kernels: 11.9 us -> 5.31 us  [edges(): pl.pallas_call(edges_kernel, grid=(rows // ROWS,), in_specs=[pl.BlockSpec...]
    unnamed x22 -> x30, local copies, waits for them, and re-layouts: 6.5 us -> 12.9 us
    pallas_call x1, Pallas kernels: 7.24 us -> 4.68 us  [update(): pl.pallas_call(update_kernel, grid=(rows // ROWS,), in_specs=[pl.BlockSpe...]
    pallas_call x1, Pallas kernels: 4.99 us -> 3.25 us  [gates(): pl.pallas_call(gating_kernel, grid=(rows // ROWS,), in_specs=[block, whol...]
    pallas_call x1, Pallas kernels: 4.18 us -> 2.56 us  [products(): pl.pallas_call(product_kernel, out_shape=jax.ShapeDtypeStruct((n_rows, n_...]
  transfers between devices with their start and end apart: 1 -> 1, of which waited for: 1 -> 1; matrix products, arithmetic and copies ran while one was open for 0% -> 0% of each run, Pallas kernels for 4% -> 3%
where the time goes in v2:
time: 120 us
  blocking collectives  63.1 us (53%)
  waiting for transfers between devices  21.9 us (18%)
  Pallas kernels  15.8 us (13%)
  local copies, waits for them, and re-layouts  13.3 us (11%)
  starting transfers between devices  5.53 us (5%)
    all_to_all x1, blocking collectives, per_device(): both = lax.all_to_all(both, axes, 0, 0, tiled=True)  63.1 us
    all_to_all x1, waiting for transfers between devices, per_device(): product = lax.all_to_all(product, axes, 0, 0, tiled=True)  21.9 us
    unnamed x30, local copies, waits for them, and re-layouts  12.9 us
    all_to_all x1, starting transfers between devices, per_device(): product = lax.all_to_all(product, axes, 0, 0, tiled=True)  5.53 us
    pallas_call x1, Pallas kernels, edges(): pl.pallas_call(edges_kernel, grid=(rows // ROWS,), in_specs=[pl.BlockSpec...  5.31 us
    pallas_call x1, Pallas kernels, update(): pl.pallas_call(update_kernel, grid=(rows // ROWS,), in_specs=[pl.BlockSpe...  4.68 us
    pallas_call x1, Pallas kernels, gates(): pl.pallas_call(gating_kernel, grid=(rows // ROWS,), in_specs=[block, whol...  3.25 us
    pallas_call x1, Pallas kernels, products(): pl.pallas_call(product_kernel, out_shape=jax.ShapeDtypeStruct((n_rows, n_...  2.56 us
  transfers between devices with their start and end apart: 1, of which 1 were waited for; matrix products, arithmetic and copies ran while one was open for 0% of the time, Pallas kernels for 3%

profile of v2, /device:TPU:0, one launch (start us, length us, event | category | flops | bytes accessed | tf_op | source)
XLA Modules:
  0.0 119.8 jit_solution(15524537557896162939)
XLA Ops:
  0.0 0.0 copy-start
  0.0 2.2 %copy-done = f32[64,128,128]{2,1,0:T(8,128)S(1)} copy-done((f32[64,128,128]{2,1,0:T(8,128)S(1)}, f32[64,128,128]{2,1,0:T(8,128)}, u32[]{:S(2)}) %copy-start) | copy-done | bytes 4194328
  2.2 0.0 copy-start.5
  2.2 0.8 copy-done.5
  3.0 0.0 copy-start.6
  3.0 0.8 copy-done.6
  3.9 0.0 copy-start.9
  3.9 0.7 copy-done.9
  4.5 0.0 copy-start.11
  4.5 0.7 copy-done.11
  5.2 5.3 %edges.1 = bf16[128,2,64,128]{3,2,1,0:T(8,128)(2,1)S(1)} custom-call(f32[64,128,128]{2,1,0:T(8,128)S(1)} %copy-done, f32[1,128]{1,0:T(1,128)S(1)} %bitcast.8, f32[1,128]{1,0:T(1,128)S(1)} %bitcast.10, bf16[128,256]{1,0:T(8,128)(2,1)S(1)} %copy-done.5, bf16[128,256]{1,0:T(8,128)(2,1)S(1)} %copy-done.6), custom_call_target="tpu_custom_call" | custom-call | flops 1073741824 | bytes 8388608 | tf_op jit(solution)/shard_map/edges/pallas_call | solution.py:55
  10.5 63.1 %all_to_all.10 = bf16[128,128,128]{2,1,0:T(8,128)(2,1)S(1)} all-to-all(bf16[128,128,128]{2,1,0:T(8,128)(2,1)S(1)} %bitcast.5), channel_id=1, replica_groups=mesh['row'=16,'col'=8] {'row','col'}, dimensions={0} | all-to-all | bytes 8388608 | tf_op jit(solution)/shard_map/all_to_all | solution.py:191
  73.6 0.0 copy-start.7
  73.6 0.0 copy-start.10
  73.6 0.0 copy-start.12
  73.6 2.6 %products.1 = bf16[16,8,64,128]{3,2,1,0:T(8,128)(2,1)S(1)} custom-call(bf16[16,8,2,64,128]{4,3,2,1,0:T(8,128)(2,1)S(1)} %bitcast.6), custom_call_target="tpu_custom_call" | custom-call | flops 2147483648 | bytes 6291456 | tf_op jit(solution)/shard_map/products/pallas_call | solution.py:127
  76.2 0.0 copy-start.4
  76.2 1.3 %copy-done.4 = bf16[16,8,64,128]{3,2,1,0:T(8,128)(2,1)} copy-done((bf16[16,8,64,128]{3,2,1,0:T(8,128)(2,1)}, bf16[16,8,64,128]{3,2,1,0:T(8,128)(2,1)S(1)}, u32[]{:S(2)}) %copy-start.4) | copy-done | bytes 2097176
  77.5 5.5 %all-to-all-start.1 = ((bf16[128,64,128]{2,1,0:T(8,128)(2,1)}), bf16[128,64,128]{2,1,0:T(8,128)(2,1)S(1)}, u32[]{:S(2)}, u32[]{:S(2)}) async-start(bf16[128,64,128]{2,1,0:T(8,128)(2,1)} %bitcast.7), calls=%async_computation.1 | async-start | bytes 4194304 | tf_op jit(solution)/shard_map/all_to_all | solution.py:193
  83.1 0.0 copy-done.7
  83.1 0.0 copy-done.10
  83.1 0.0 copy-done.12
  83.1 0.0 copy-start.1
  83.1 2.2 %copy-done.1 = f32[64,128,128]{2,1,0:T(8,128)S(1)} copy-done((f32[64,128,128]{2,1,0:T(8,128)S(1)}, f32[64,128,128]{2,1,0:T(8,128)}, u32[]{:S(2)}) %copy-start.1) | copy-done | bytes 4194328
  85.3 0.0 copy-start.13
  85.3 0.0 copy-start.14
  85.3 0.0 copy-start.8
  85.3 3.2 %gates.1.gating = f32[64,128,128]{2,1,0:T(8,128)S(1)} custom-call(f32[64,128,128]{2,1,0:T(8,128)S(1)} %copy-done.1, f32[1,128]{1,0:T(1,128)S(1)} %bitcast.9, f32[1,128]{1,0:T(1,128)S(1)} %bitcast.11, bf16[128,128]{1,0:T(8,128)(2,1)S(1)} %copy-done.7), custom_call_target="tpu_custom_call" | custom-call | flops 268435456 | bytes 8388608 | tf_op jit(solution)/shard_map/gates/pallas_call | solution.py:90
  88.5 0.0 copy-start.2
  88.5 2.0 %copy-done.2 = f32[64,128,128]{2,1,0:T(8,128)} copy-done((f32[64,128,128]{2,1,0:T(8,128)}, f32[64,128,128]{2,1,0:T(8,128)S(1)}, u32[]{:S(2)}) %copy-start.2) | copy-done | bytes 4194328
  90.6 21.9 %all-to-all-done.1.product = bf16[128,64,128]{2,1,0:T(8,128)(2,1)S(1)} async-done(((bf16[128,64,128]{2,1,0:T(8,128)(2,1)}), bf16[128,64,128]{2,1,0:T(8,128)(2,1)S(1)}, u32[]{:S(2)}, u32[]{:S(2)}) %all-to-all-start.1) | async-done | bytes 2097184 | tf_op jit(solution)/shard_map/all_to_all | solution.py:193
  112.5 0.0 copy-done.13
  112.5 0.2 broadcast_in_dim.20.gain
  112.7 0.0 copy-done.14
  112.7 0.2 broadcast_in_dim.21.bias
  112.9 0.0 copy-done.8
  112.9 0.0 copy-start.3
  112.9 2.2 %copy-done.3 = f32[64,128,128]{2,1,0:T(8,128)S(1)} copy-done((f32[64,128,128]{2,1,0:T(8,128)S(1)}, f32[64,128,128]{2,1,0:T(8,128)}, u32[]{:S(2)}) %copy-start.3) | copy-done | bytes 4194328
  115.1 4.7 %update.1 = f32[64,128,128]{2,1,0:T(8,128)} custom-call(bf16[128,64,128]{2,1,0:T(8,128)(2,1)S(1)} %all-to-all-done.1.product, f32[64,128,128]{2,1,0:T(8,128)S(1)} %copy-done.3, f32[128,1,128]{2,1,0:T(1,128)S(1)} %broadcast_in_dim.20.gain, f32[128,1,128]{2,1,0:T(1,128)S(1)} %broadcast_in_dim.21.bias, bf16[128,128]{1,0:T(8,128)(2,1)S(1)} %copy-done.8), custom_call_target="tpu_custom_call" | custom-call | flops 268435456 | bytes 10485760 | tf_op jit(solution)/shard_map/update/pallas_call | solution.py:162
Async XLA Ops:
  0.0 2.2 %copy-start = (f32[64,128,128]{2,1,0:T(8,128)S(1)}, f32[64,128,128]{2,1,0:T(8,128)}, u32[]{:S(2)}) copy-start(f32[64,128,128]{2,1,0:T(8,128)} %pair.3) | copy-start | bytes 12582916
  2.2 0.8 copy-start.5
  3.0 0.8 copy-start.6
  3.9 0.7 copy-start.9
  4.5 0.7 copy-start.11
  73.6 9.4 %copy-start.7 = (bf16[128,128]{1,0:T(8,128)(2,1)S(1)}, bf16[128,128]{1,0:T(8,128)(2,1)}, u32[]{:S(2)}) copy-start(bf16[128,128]{1,0:T(8,128)(2,1)} %weight.2) | copy-start | bytes 98308
  73.6 9.4 %copy-start.10 = (f32[128]{0:T(128)S(1)}, f32[128]{0:T(128)}, u32[]{:S(2)}) copy-start(f32[128]{0:T(128)} %param.10) | copy-start | bytes 1540
  73.6 9.5 %copy-start.12 = (f32[128]{0:T(128)S(1)}, f32[128]{0:T(128)}, u32[]{:S(2)}) copy-start(f32[128]{0:T(128)} %param.11) | copy-start | bytes 1540
  76.2 1.3 %copy-start.4 = (bf16[16,8,64,128]{3,2,1,0:T(8,128)(2,1)}, bf16[16,8,64,128]{3,2,1,0:T(8,128)(2,1)S(1)}, u32[]{:S(2)}) copy-start(bf16[16,8,64,128]{3,2,1,0:T(8,128)(2,1)S(1)} %products.1) | copy-start | bytes 6291460
  77.5 35.0 %all-to-all-start.1 = ((bf16[128,64,128]{2,1,0:T(8,128)(2,1)}), bf16[128,64,128]{2,1,0:T(8,128)(2,1)S(1)}, u32[]{:S(2)}, u32[]{:S(2)}) async-start(bf16[128,64,128]{2,1,0:T(8,128)(2,1)} %bitcast.7), calls=%async_computation.1 | async-start | bytes 4194304 | tf_op jit(solution)/shard_map/all_to_all | solution.py:193
  83.1 2.2 %copy-start.1 = (f32[64,128,128]{2,1,0:T(8,128)S(1)}, f32[64,128,128]{2,1,0:T(8,128)}, u32[]{:S(2)}) copy-start(f32[64,128,128]{2,1,0:T(8,128)} %pair.3) | copy-start | bytes 12582916
  85.3 27.2 %copy-start.13 = (f32[128]{0:T(128)S(1)}, f32[128]{0:T(128)}, u32[]{:S(2)}) copy-start(f32[128]{0:T(128)} %param.16) | copy-start | bytes 1540
  85.3 27.4 %copy-start.14 = (f32[128]{0:T(128)S(1)}, f32[128]{0:T(128)}, u32[]{:S(2)}) copy-start(f32[128]{0:T(128)} %param.17) | copy-start | bytes 1540
  85.3 27.6 %copy-start.8 = (bf16[128,128]{1,0:T(8,128)(2,1)S(1)}, bf16[128,128]{1,0:T(8,128)(2,1)}, u32[]{:S(2)}) copy-start(bf16[128,128]{1,0:T(8,128)(2,1)} %weight.3) | copy-start | bytes 98308
  88.5 2.0 %copy-start.2 = (f32[64,128,128]{2,1,0:T(8,128)}, f32[64,128,128]{2,1,0:T(8,128)S(1)}, u32[]{:S(2)}) copy-start(f32[64,128,128]{2,1,0:T(8,128)S(1)} %gates.1.gating) | copy-start | bytes 12582916
  112.9 2.2 %copy-start.3 = (f32[64,128,128]{2,1,0:T(8,128)S(1)}, f32[64,128,128]{2,1,0:T(8,128)}, u32[]{:S(2)}) copy-start(f32[64,128,128]{2,1,0:T(8,128)} %copy-done.2) | copy-start | bytes 12582916

commit v3 on v2

v3 whole, which is shorter than its diff:
```python
import jax
import jax.numpy as jnp
from jax import lax
from jax.experimental import pallas as pl
from jax.experimental.pallas import tpu as pltpu
from jax.sharding import PartitionSpec as P

F32, BF16 = jnp.float32, jnp.bfloat16
EPS = 1e-05
ROWS = 16
PAD = 4


def in_hbm(*arrays):
    return [pltpu.with_memory_space_constraint(array, pltpu.HBM) for array in arrays]


def sigmoid(values):
    return 0.5 * jnp.tanh(0.5 * values) + 0.5


def normalize(values, gain, bias):
    center = jnp.mean(values, axis=-1, keepdims=True)
    values = values - center
    spread = jnp.mean(values * values, axis=-1, keepdims=True)
    return (values * lax.rsqrt(spread + EPS) * gain + bias).astype(BF16)


def edges_kernel(
    pair_far, gain_far, bias_far, left_far, right_far, out,
    pair, gain, bias, w_left, w_right, weight, left_rows, right_rows, sems,
):
    rows, tokens, channels = pair.shape
    pitch = channels + PAD
    small = [
        pltpu.make_async_copy(far, near, sems.at[place])
        for place, (far, near) in enumerate(
            [(gain_far, gain), (bias_far, bias), (left_far, w_left), (right_far, w_right)]
        )
    ]

    def fetch(step):
        place = pl.ds(step * ROWS, ROWS)
        return pltpu.make_async_copy(pair_far.at[place], pair.at[place], sems.at[4 + step])

    fetch(0).start()
    for copy in small:
        copy.start()
    for step in range(1, rows // ROWS):
        fetch(step).start()
    for copy in small:
        copy.wait()
    weight[: 2 * channels] = w_left[...].T
    weight[2 * channels :] = w_right[...].T

    def body(step, carry):
        fetch(step).wait()
        base = pl.multiple_of(step * ROWS, ROWS)
        for row in range(0, ROWS, 2):
            values = pair[pl.ds(base + row, 2)].reshape(2 * tokens, channels)
            normed = normalize(values, gain[...], bias[...])
            projected = lax.dot_general(
                weight[...], normed, (((1,), (1,)), ((), ())), preferred_element_type=F32
            )
            lefts = sigmoid(projected[:channels]) * projected[channels : 2 * channels]
            rights = sigmoid(projected[2 * channels : 3 * channels]) * projected[3 * channels :]
            for half in range(2):
                place = pl.ds((row + half) * pitch, channels)
                lanes = slice(half * tokens, (half + 1) * tokens)
                left_rows[place, :] = lefts[:, lanes]
                right_rows[place, :] = rights[:, lanes]
        for channel in range(channels):
            place = pl.ds(channel, ROWS, stride=pitch)
            out[channel, 0, pl.ds(base, ROWS), :] = left_rows[place, :].astype(BF16)
            out[channel, 1, pl.ds(base, ROWS), :] = right_rows[place, :].astype(BF16)
        return carry

    lax.fori_loop(0, rows // ROWS, body, 0)


def edges(pair, gain, bias, w_left, w_right):
    rows, tokens, channels = pair.shape
    far = pl.BlockSpec(memory_space=pltpu.HBM)
    return pl.pallas_call(
        edges_kernel,
        in_specs=[far] * 5,
        out_specs=pl.BlockSpec(memory_space=pltpu.VMEM),
        out_shape=jax.ShapeDtypeStruct((channels, 2, rows, tokens), BF16),
        scratch_shapes=[
            pltpu.VMEM(pair.shape, F32),
            pltpu.VMEM(gain.shape, F32),
            pltpu.VMEM(bias.shape, F32),
            pltpu.VMEM(w_left.shape, BF16),
            pltpu.VMEM(w_right.shape, BF16),
            pltpu.VMEM((4 * channels, channels), BF16),
            pltpu.VMEM((ROWS * (channels + PAD), tokens), F32),
            pltpu.VMEM((ROWS * (channels + PAD), tokens), F32),
            pltpu.SemaphoreType.DMA((4 + rows // ROWS,)),
        ],
        compiler_params=pltpu.CompilerParams(vmem_limit_bytes=20 * 2**20),
        cost_estimate=pl.CostEstimate(
            flops=8 * rows * tokens * channels * channels,
            bytes_accessed=8 * rows * tokens * channels,
            transcendentals=2 * rows * tokens * channels,
        ),
        name="edges",
    )(*in_hbm(pair, gain, bias, w_left, w_right))


def gating_kernel(pair, gain, bias, weight, gating):
    rows, tokens, channels = pair.shape
    normed = normalize(pair[...].reshape(rows * tokens, channels), gain[...], bias[...])
    projected = jnp.dot(normed, weight[...], preferred_element_type=F32)
    gating[...] = sigmoid(projected).reshape(rows, tokens, channels)


def gates(pair, gain, bias, weight):
    rows, tokens, channels = pair.shape
    whole = lambda *shape: pl.BlockSpec(shape, lambda step: (0,) * len(shape))
    block = pl.BlockSpec((ROWS, tokens, channels), lambda step: (step, 0, 0))
    return pl.pallas_call(
        gating_kernel,
        grid=(rows // ROWS,),
        in_specs=[block, whole(1, channels), whole(1, channels), whole(channels, channels)],
        out_specs=block,
        out_shape=jax.ShapeDtypeStruct(pair.shape, F32),
        compiler_params=pltpu.CompilerParams(vmem_limit_bytes=16 * 2**20),
        cost_estimate=pl.CostEstimate(
            flops=2 * rows * tokens * channels * channels,
            bytes_accessed=8 * rows * tokens * channels,
            transcendentals=rows * tokens * channels,
        ),
        name="gates",
    )(pair, gain, bias, weight)


def product_kernel(both, out_far, left_turned, right_whole, out, sems):
    n_rows, n_cols, _, depth, tokens = both.shape
    for col in range(n_cols):
        lanes = slice(col * tokens, (col + 1) * tokens)
        for row in range(n_rows):
            right_whole[row * depth : (row + 1) * depth, lanes] = both[row, col, 1]
        column = jnp.concatenate([both[row, col, 0] for row in range(n_rows)], axis=0)
        left_turned[lanes, :] = column.T
    copies = []
    for col in range(0, n_cols, 2):
        total = jnp.dot(
            left_turned[...],
            right_whole[:, col * tokens : (col + 2) * tokens],
            preferred_element_type=F32,
        ).astype(BF16)
        for part in range(2):
            block = total[:, part * tokens : (part + 1) * tokens]
            out[:, col + part] = block.reshape(n_rows, depth, tokens)
        place = pl.ds(col, 2)
        copies.append(
            pltpu.make_async_copy(out.at[:, place], out_far.at[:, place], sems.at[col // 2])
        )
        copies[-1].start()
    for copy in copies:
        copy.wait()


def products(both):
    n_rows, n_cols, _, depth, tokens = both.shape
    size = n_rows * depth
    shape = (n_rows, n_cols, depth, tokens)
    return pl.pallas_call(
        product_kernel,
        in_specs=[pl.BlockSpec(memory_space=pltpu.VMEM)],
        out_specs=pl.BlockSpec(memory_space=pltpu.HBM),
        out_shape=jax.ShapeDtypeStruct(shape, BF16),
        scratch_shapes=[pltpu.VMEM((size, size), BF16)] * 2
        + [pltpu.VMEM(shape, BF16), pltpu.SemaphoreType.DMA((n_cols // 2,))],
        compiler_params=pltpu.CompilerParams(vmem_limit_bytes=24 * 2**20),
        cost_estimate=pl.CostEstimate(
            flops=2 * size**3, bytes_accessed=6 * size * size, transcendentals=0
        ),
        name="products",
    )(both)


def update_kernel(
    product, gating_far, gain_far, bias_far, weight_far, out_far,
    gating, gain, bias, weight, gains, biases, rows_of, out, sems,
):
    channels, rows, tokens = product.shape
    pitch = ROWS + PAD
    steps = rows // ROWS
    small = [
        pltpu.make_async_copy(far, near, sems.at[place])
        for place, (far, near) in enumerate(
            [(gain_far, gain), (bias_far, bias), (weight_far, weight)]
        )
    ]

    def fetch(step):
        place = pl.ds(step * ROWS, ROWS)
        return pltpu.make_async_copy(gating_far.at[place], gating.at[place], sems.at[3 + step])

    def send(step):
        place = pl.ds(step * ROWS, ROWS)
        return pltpu.make_async_copy(out.at[place], out_far.at[place], sems.at[3 + steps + step])

    for copy in small:
        copy.start()
    for step in range(steps):
        fetch(step).start()
    for copy in small:
        copy.wait()
    gains[...] = jnp.broadcast_to(gain[...], (tokens, channels)).T
    biases[...] = jnp.broadcast_to(bias[...], (tokens, channels)).T

    def body(step, carry):
        base = pl.multiple_of(step * ROWS, ROWS)
        load = lambda channel: product[channel, pl.ds(base, ROWS), :].astype(F32)
        center = load(0)
        for channel in range(1, channels):
            center = center + load(channel)
        center = center * (1.0 / channels)
        spread = jnp.zeros_like(center)
        for channel in range(channels):
            offset = load(channel) - center
            spread = spread + offset * offset
        scale = lax.rsqrt(spread * (1.0 / channels) + EPS)
        for channel in range(channels):
            normed = (load(channel) - center) * scale
            normed = normed * gains[channel : channel + 1, :] + biases[channel : channel + 1, :]
            rows_of[pl.ds(channel * pitch, ROWS), :] = normed
        fetch(step).wait()
        for row in range(ROWS):
            normed = rows_of[pl.ds(row, channels, stride=pitch), :].astype(BF16)
            projected = lax.dot_general(
                normed, weight[...], (((0,), (0,)), ((), ())), preferred_element_type=F32
            )
            out[base + row] = gating[base + row] * projected
        send(step).start()
        return carry

    lax.fori_loop(0, steps, body, 0)
    for step in range(steps):
        send(step).wait()


def update(product, gating, gain, bias, weight):
    channels, rows, tokens = product.shape
    far = pl.BlockSpec(memory_space=pltpu.HBM)
    return pl.pallas_call(
        update_kernel,
        in_specs=[pl.BlockSpec(memory_space=pltpu.VMEM), far, far, far, far],
        out_specs=far,
        out_shape=jax.ShapeDtypeStruct((rows, tokens, channels), F32),
        scratch_shapes=[
            pltpu.VMEM(gating.shape, F32),
            pltpu.VMEM(gain.shape, F32),
            pltpu.VMEM(bias.shape, F32),
            pltpu.VMEM(weight.shape, BF16),
            pltpu.VMEM((channels, tokens), F32),
            pltpu.VMEM((channels, tokens), F32),
            pltpu.VMEM((channels * (ROWS + PAD), tokens), F32),
            pltpu.VMEM((rows, tokens, channels), F32),
            pltpu.SemaphoreType.DMA((3 + 2 * (rows // ROWS),)),
        ],
        compiler_params=pltpu.CompilerParams(vmem_limit_bytes=20 * 2**20),
        cost_estimate=pl.CostEstimate(
            flops=2 * rows * tokens * channels * channels,
            bytes_accessed=10 * rows * tokens * channels,
            transcendentals=0,
        ),
        name="update",
    )(product, *in_hbm(gating, gain, bias, weight))


def per_device(n_rows, n_cols, pair, ln_gain, ln_bias, w_left, w_right, w_gate, w_out, out_gain, out_bias):
    rows, tokens, channels = pair.shape
    axes = ("row", "col")
    gain, bias = ln_gain[None], ln_bias[None]
    both = edges(pair, gain, bias, w_left, w_right).reshape(channels, 2 * rows, tokens)
    gating = gates(pair, gain, bias, w_gate)
    both = lax.all_to_all(both, axes, 0, 0, tiled=True)
    product = products(both.reshape(n_rows, n_cols, 2, rows, tokens)).reshape(channels, rows, tokens)
    product = lax.all_to_all(product, axes, 0, 0, tiled=True)
    return update(product, gating, out_gain[None], out_bias[None], w_out)


def solution(mesh):
    n_rows, n_cols = mesh.shape["row"], mesh.shape["col"]
    return jax.shard_map(
        lambda *args: per_device(n_rows, n_cols, *args),
        mesh=mesh,
        in_specs=(P("row", "col", None), P(), P(), P(), P(), P(), P(), P(), P()),
        out_specs=P("row", "col", None),
        check_vma=False,
    )
```

time: 120 us -> 117 us (0.975)
  local copies, waits for them, and re-layouts: 13.3 us -> 5.44 us
  Pallas kernels: 15.8 us -> 20.6 us
    unnamed x30 -> x12, local copies, waits for them, and re-layouts: 12.9 us -> 5.44 us
    pallas_call x3, Pallas kernels: 12.6 us -> 17.3 us  [the longest x1 6.25 us: edges(): pl.pallas_call(edges_kernel, in_specs=[far] * 5, out_specs=pl.BlockSpec(m...]
where the time goes in v3:
time: 117 us
  blocking collectives  63.1 us (54%)
  waiting for transfers between devices  22 us (19%)
  Pallas kernels  20.6 us (18%)
  starting transfers between devices  5.52 us (5%)
  local copies, waits for them, and re-layouts  5.44 us (5%)
    all_to_all x1, blocking collectives, per_device(): both = lax.all_to_all(both, axes, 0, 0, tiled=True)  63.1 us
    all_to_all x1, waiting for transfers between devices, per_device(): product = lax.all_to_all(product, axes, 0, 0, tiled=True)  22 us
    pallas_call x1, Pallas kernels, edges(): pl.pallas_call(edges_kernel, in_specs=[far] * 5, out_specs=pl.BlockSpec(m...  6.25 us
    pallas_call x1, Pallas kernels, products(): pl.pallas_call(product_kernel, in_specs=[pl.BlockSpec(memory_space=pltpu....  5.63 us
    all_to_all x1, starting transfers between devices, per_device(): product = lax.all_to_all(product, axes, 0, 0, tiled=True)  5.52 us
    unnamed x12, local copies, waits for them, and re-layouts  5.44 us
    pallas_call x1, Pallas kernels, update(): pl.pallas_call(update_kernel, in_specs=[pl.BlockSpec(memory_space=pltpu.V...  5.43 us
    pallas_call x1, Pallas kernels, gates(): pl.pallas_call(gating_kernel, grid=(rows // ROWS,), in_specs=[block, whol...  3.25 us
  transfers between devices with their start and end apart: 1, of which 1 were waited for; matrix products, arithmetic and copies ran while one was open for 0% of the time, Pallas kernels for 3%

profile of v3, /device:TPU:0, one launch (start us, length us, event | category | flops | bytes accessed | tf_op | source)
XLA Modules:
  0.0 116.7 jit_solution(13069694018973948470)
XLA Ops:
  0.0 6.3 %edges.1 = bf16[128,2,64,128]{3,2,1,0:T(8,128)(2,1)S(1)} custom-call(f32[64,128,128]{2,1,0:T(8,128)} %pair.1, f32[1,128]{1,0:T(1,128)} %bitcast.10, f32[1,128]{1,0:T(1,128)} %bitcast.12, bf16[128,256]{1,0:T(8,128)(2,1)} %left_far.1, bf16[128,256]{1,0:T(8,128)(2,1)} %right_far.1), custom_call_target="tpu_custom_call" | custom-call | flops 1073741824 | bytes 8388608 | tf_op jit(solution)/shard_map/edges/pallas_call | solution.py:84
  6.3 63.1 %all_to_all.10 = bf16[128,128,128]{2,1,0:T(8,128)(2,1)S(1)} all-to-all(bf16[128,128,128]{2,1,0:T(8,128)(2,1)S(1)} %bitcast.7), channel_id=1, replica_groups=mesh['row'=16,'col'=8] {'row','col'}, dimensions={0} | all-to-all | bytes 8388608 | tf_op jit(solution)/shard_map/all_to_all | solution.py:280
  69.4 0.0 copy-start.3
  69.4 0.0 copy-start.4
  69.4 0.0 copy-start.5
  69.4 5.6 %products.1 = bf16[16,8,64,128]{3,2,1,0:T(8,128)(2,1)S(1)} custom-call(bf16[16,8,2,64,128]{4,3,2,1,0:T(8,128)(2,1)S(1)} %bitcast.8), custom_call_target="tpu_custom_call" | custom-call | flops 2147483648 | bytes 6291456 | tf_op jit(solution)/shard_map/products/pallas_call | solution.py:168
  75.0 0.0 copy-start.2
  75.0 1.3 %copy-done.2 = bf16[16,8,64,128]{3,2,1,0:T(8,128)(2,1)} copy-done((bf16[16,8,64,128]{3,2,1,0:T(8,128)(2,1)}, bf16[16,8,64,128]{3,2,1,0:T(8,128)(2,1)S(1)}, u32[]{:S(2)}) %copy-start.2) | copy-done | bytes 2097176
  76.3 5.5 %all-to-all-start.1 = ((bf16[128,64,128]{2,1,0:T(8,128)(2,1)}), bf16[128,64,128]{2,1,0:T(8,128)(2,1)S(1)}, u32[]{:S(2)}, u32[]{:S(2)}) async-start(bf16[128,64,128]{2,1,0:T(8,128)(2,1)} %bitcast.9), calls=%async_computation.1 | async-start | bytes 4194304 | tf_op jit(solution)/shard_map/all_to_all | solution.py:282
  81.9 0.0 copy-done.3
  81.9 0.0 copy-done.4
  81.9 0.0 copy-done.5
  81.9 0.0 copy-start
  81.9 2.2 %copy-done = f32[64,128,128]{2,1,0:T(8,128)S(1)} copy-done((f32[64,128,128]{2,1,0:T(8,128)S(1)}, f32[64,128,128]{2,1,0:T(8,128)}, u32[]{:S(2)}) %copy-start) | copy-done | bytes 4194328
  84.1 3.2 %gates.1.gating_far = f32[64,128,128]{2,1,0:T(8,128)S(1)} custom-call(f32[64,128,128]{2,1,0:T(8,128)S(1)} %copy-done, f32[1,128]{1,0:T(1,128)S(1)} %bitcast.11, f32[1,128]{1,0:T(1,128)S(1)} %bitcast.13, bf16[128,128]{1,0:T(8,128)(2,1)S(1)} %copy-done.3), custom_call_target="tpu_custom_call" | custom-call | flops 268435456 | bytes 8388608 | tf_op jit(solution)/shard_map/gates/pallas_call | solution.py:121
  87.3 0.0 copy-start.1
  87.4 1.9 %copy-done.1 = f32[64,128,128]{2,1,0:T(8,128)} copy-done((f32[64,128,128]{2,1,0:T(8,128)}, f32[64,128,128]{2,1,0:T(8,128)S(1)}, u32[]{:S(2)}) %copy-start.1) | copy-done | bytes 4194328
  89.3 22.0 %all-to-all-done.1.product = bf16[128,64,128]{2,1,0:T(8,128)(2,1)S(1)} async-done(((bf16[128,64,128]{2,1,0:T(8,128)(2,1)}), bf16[128,64,128]{2,1,0:T(8,128)(2,1)S(1)}, u32[]{:S(2)}, u32[]{:S(2)}) %all-to-all-start.1) | async-done | bytes 2097184 | tf_op jit(solution)/shard_map/all_to_all | solution.py:282
  111.3 5.4 %update.1 = f32[64,128,128]{2,1,0:T(8,128)} custom-call(bf16[128,64,128]{2,1,0:T(8,128)(2,1)S(1)} %all-to-all-done.1.product, f32[64,128,128]{2,1,0:T(8,128)} %copy-done.1, f32[1,128]{1,0:T(1,128)} %bitcast.14, f32[1,128]{1,0:T(1,128)} %bitcast.15, bf16[128,128]{1,0:T(8,128)(2,1)} %weight_far.1), custom_call_target="tpu_custom_call" | custom-call | flops 268435456 | bytes 10485760 | tf_op jit(solution)/shard_map/update/pallas_call | solution.py:248
Async XLA Ops:
  69.4 12.5 %copy-start.3 = (bf16[128,128]{1,0:T(8,128)(2,1)S(1)}, bf16[128,128]{1,0:T(8,128)(2,1)}, u32[]{:S(2)}) copy-start(bf16[128,128]{1,0:T(8,128)(2,1)} %weight.1) | copy-start | bytes 98308
  69.4 12.5 %copy-start.4 = (f32[128]{0:T(128)S(1)}, f32[128]{0:T(128)}, u32[]{:S(2)}) copy-start(f32[128]{0:T(128)} %param.10) | copy-start | bytes 1540
  69.4 12.5 %copy-start.5 = (f32[128]{0:T(128)S(1)}, f32[128]{0:T(128)}, u32[]{:S(2)}) copy-start(f32[128]{0:T(128)} %param.11) | copy-start | bytes 1540
  75.0 1.3 %copy-start.2 = (bf16[16,8,64,128]{3,2,1,0:T(8,128)(2,1)}, bf16[16,8,64,128]{3,2,1,0:T(8,128)(2,1)S(1)}, u32[]{:S(2)}) copy-start(bf16[16,8,64,128]{3,2,1,0:T(8,128)(2,1)S(1)} %products.1) | copy-start | bytes 6291460
  76.3 35.0 %all-to-all-start.1 = ((bf16[128,64,128]{2,1,0:T(8,128)(2,1)}), bf16[128,64,128]{2,1,0:T(8,128)(2,1)S(1)}, u32[]{:S(2)}, u32[]{:S(2)}) async-start(bf16[128,64,128]{2,1,0:T(8,128)(2,1)} %bitcast.9), calls=%async_computation.1 | async-start | bytes 4194304 | tf_op jit(solution)/shard_map/all_to_all | solution.py:282
  81.9 2.2 %copy-start = (f32[64,128,128]{2,1,0:T(8,128)S(1)}, f32[64,128,128]{2,1,0:T(8,128)}, u32[]{:S(2)}) copy-start(f32[64,128,128]{2,1,0:T(8,128)} %pair.1) | copy-start | bytes 12582916
  87.3 1.9 %copy-start.1 = (f32[64,128,128]{2,1,0:T(8,128)}, f32[64,128,128]{2,1,0:T(8,128)S(1)}, u32[]{:S(2)}) copy-start(f32[64,128,128]{2,1,0:T(8,128)S(1)} %gates.1.gating_far) | copy-start | bytes 12582916

commit v4 on v3

--- a/solution.py
+++ b/solution.py
@@ -53,15 +53,19 @@
     weight[: 2 * channels] = w_left[...].T
     weight[2 * channels :] = w_right[...].T
 
+    gains = jnp.broadcast_to(gain[...], (2 * tokens, channels)).T
+    biases = jnp.broadcast_to(bias[...], (2 * tokens, channels)).T
+
     def body(step, carry):
         fetch(step).wait()
         base = pl.multiple_of(step * ROWS, ROWS)
         for row in range(0, ROWS, 2):
-            values = pair[pl.ds(base + row, 2)].reshape(2 * tokens, channels)
-            normed = normalize(values, gain[...], bias[...])
-            projected = lax.dot_general(
-                weight[...], normed, (((1,), (1,)), ((), ())), preferred_element_type=F32
-            )
+            values = pair[pl.ds(base + row, 2)].reshape(2 * tokens, channels).T
+            center = jnp.sum(values, axis=0, keepdims=True) * (1.0 / channels)
+            values = values - center
+            spread = jnp.sum(values * values, axis=0, keepdims=True) * (1.0 / channels)
+            normed = values * lax.rsqrt(spread + EPS) * gains + biases
+            projected = jnp.dot(weight[...], normed.astype(BF16), preferred_element_type=F32)
             lefts = sigmoid(projected[:channels]) * projected[channels : 2 * channels]
             rights = sigmoid(projected[2 * channels : 3 * channels]) * projected[3 * channels :]
             for half in range(2):
@@ -169,7 +173,7 @@
         product_kernel,
         in_specs=[pl.BlockSpec(memory_space=pltpu.VMEM)],
         out_specs=pl.BlockSpec(memory_space=pltpu.HBM),
-        out_shape=jax.ShapeDtypeStruct(shape, BF16),
+        out_shape=pltpu.HBM(shape, BF16),
         scratch_shapes=[pltpu.VMEM((size, size), BF16)] * 2
         + [pltpu.VMEM(shape, BF16), pltpu.SemaphoreType.DMA((n_cols // 2,))],
         compiler_params=pltpu.CompilerParams(vmem_limit_bytes=24 * 2**20),
@@ -181,33 +185,21 @@
 
 
 def update_kernel(
-    product, gating_far, gain_far, bias_far, weight_far, out_far,
-    gating, gain, bias, weight, gains, biases, rows_of, out, sems,
+    product, gating_far, gain, bias, weight, out_far, gating, gains, biases, rows_of, out, sems
 ):
     channels, rows, tokens = product.shape
     pitch = ROWS + PAD
     steps = rows // ROWS
-    small = [
-        pltpu.make_async_copy(far, near, sems.at[place])
-        for place, (far, near) in enumerate(
-            [(gain_far, gain), (bias_far, bias), (weight_far, weight)]
-        )
-    ]
-
     def fetch(step):
         place = pl.ds(step * ROWS, ROWS)
-        return pltpu.make_async_copy(gating_far.at[place], gating.at[place], sems.at[3 + step])
+        return pltpu.make_async_copy(gating_far.at[place], gating.at[place], sems.at[step])
 
     def send(step):
         place = pl.ds(step * ROWS, ROWS)
-        return pltpu.make_async_copy(out.at[place], out_far.at[place], sems.at[3 + steps + step])
-
-    for copy in small:
-        copy.start()
+        return pltpu.make_async_copy(out.at[place], out_far.at[place], sems.at[steps + step])
+
     for step in range(steps):
         fetch(step).start()
-    for copy in small:
-        copy.wait()
     gains[...] = jnp.broadcast_to(gain[...], (tokens, channels)).T
     biases[...] = jnp.broadcast_to(bias[...], (tokens, channels)).T
 
@@ -244,22 +236,19 @@
 
 def update(product, gating, gain, bias, weight):
     channels, rows, tokens = product.shape
-    far = pl.BlockSpec(memory_space=pltpu.HBM)
+    near, far = pl.BlockSpec(memory_space=pltpu.VMEM), pl.BlockSpec(memory_space=pltpu.HBM)
     return pl.pallas_call(
         update_kernel,
-        in_specs=[pl.BlockSpec(memory_space=pltpu.VMEM), far, far, far, far],
+        in_specs=[near, far, near, near, near],
         out_specs=far,
         out_shape=jax.ShapeDtypeStruct((rows, tokens, channels), F32),
         scratch_shapes=[
             pltpu.VMEM(gating.shape, F32),
-            pltpu.VMEM(gain.shape, F32),
-            pltpu.VMEM(bias.shape, F32),
-            pltpu.VMEM(weight.shape, BF16),
             pltpu.VMEM((channels, tokens), F32),
             pltpu.VMEM((channels, tokens), F32),
             pltpu.VMEM((channels * (ROWS + PAD), tokens), F32),
             pltpu.VMEM((rows, tokens, channels), F32),
-            pltpu.SemaphoreType.DMA((3 + 2 * (rows // ROWS),)),
+            pltpu.SemaphoreType.DMA((2 * (rows // ROWS),)),
         ],
         compiler_params=pltpu.CompilerParams(vmem_limit_bytes=20 * 2**20),
         cost_estimate=pl.CostEstimate(
@@ -268,7 +257,7 @@
             transcendentals=0,
         ),
         name="update",
-    )(product, *in_hbm(gating, gain, bias, weight))
+    )(product, *in_hbm(gating), gain, bias, weight)
 
 
 def per_device(n_rows, n_cols, pair, ln_gain, ln_bias, w_left, w_right, w_gate, w_out, out_gain, out_bias):

time: 117 us -> 113 us (0.966)
  Pallas kernels: 20.6 us -> 17.9 us
  local copies, waits for them, and re-layouts: 5.44 us -> 4.15 us
    pallas_call x1, Pallas kernels: 5.63 us -> 3.69 us  [products(): pl.pallas_call(product_kernel, in_specs=[pl.BlockSpec(memory_space=pltpu....]
    unnamed x12 -> x16, local copies, waits for them, and re-layouts: 5.44 us -> 4.15 us
where the time goes in v4:
time: 113 us
  blocking collectives  63.1 us (56%)
  waiting for transfers between devices  22 us (19%)
  Pallas kernels  17.9 us (16%)
  starting transfers between devices  5.53 us (5%)
  local copies, waits for them, and re-layouts  4.15 us (4%)
    all_to_all x1, blocking collectives, per_device(): both = lax.all_to_all(both, axes, 0, 0, tiled=True)  63.1 us
    all_to_all x1, waiting for transfers between devices, per_device(): product = lax.all_to_all(product, axes, 0, 0, tiled=True)  22 us
    pallas_call x1, Pallas kernels, edges(): pl.pallas_call(edges_kernel, in_specs=[far] * 5, out_specs=pl.BlockSpec(m...  5.75 us
    all_to_all x1, starting transfers between devices, per_device(): product = lax.all_to_all(product, axes, 0, 0, tiled=True)  5.53 us
    pallas_call x1, Pallas kernels, update(): pl.pallas_call(update_kernel, in_specs=[near, far, near, near, near], out...  5.21 us
    unnamed x16, local copies, waits for them, and re-layouts  4.15 us
    pallas_call x1, Pallas kernels, products(): pl.pallas_call(product_kernel, in_specs=[pl.BlockSpec(memory_space=pltpu....  3.69 us
    pallas_call x1, Pallas kernels, gates(): pl.pallas_call(gating_kernel, grid=(rows // ROWS,), in_specs=[block, whol...  3.25 us
  transfers between devices with their start and end apart: 1, of which 1 were waited for; matrix products, arithmetic and copies ran while one was open for 0% of the time, Pallas kernels for 3%

profile of v4, /device:TPU:0, one launch (start us, length us, event | category | flops | bytes accessed | tf_op | source)
XLA Modules:
  0.0 112.7 jit_solution(18376998298272242146)
XLA Ops:
  0.0 5.7 %edges.1 = bf16[128,2,64,128]{3,2,1,0:T(8,128)(2,1)S(1)} custom-call(f32[64,128,128]{2,1,0:T(8,128)} %pair.1, f32[1,128]{1,0:T(1,128)} %bitcast.9, f32[1,128]{1,0:T(1,128)} %bitcast.11, bf16[128,256]{1,0:T(8,128)(2,1)} %left_far.1, bf16[128,256]{1,0:T(8,128)(2,1)} %right_far.1), custom_call_target="tpu_custom_call" | custom-call | flops 1073741824 | bytes 8388608 | tf_op jit(solution)/shard_map/edges/pallas_call | solution.py:88
  5.8 63.1 %all_to_all.10 = bf16[128,128,128]{2,1,0:T(8,128)(2,1)S(1)} all-to-all(bf16[128,128,128]{2,1,0:T(8,128)(2,1)S(1)} %bitcast.7), channel_id=1, replica_groups=mesh['row'=16,'col'=8] {'row','col'}, dimensions={0} | all-to-all | bytes 8388608 | tf_op jit(solution)/shard_map/all_to_all | solution.py:269
  68.9 0.0 copy-start.2
  68.9 0.0 copy-start.4
  68.9 0.0 copy-start.5
  68.9 3.7 %products.1 = bf16[16,8,64,128]{3,2,1,0:T(8,128)(2,1)} custom-call(bf16[16,8,2,64,128]{4,3,2,1,0:T(8,128)(2,1)S(1)} %bitcast.8), custom_call_target="tpu_custom_call" | custom-call | flops 2147483648 | bytes 6291456 | tf_op jit(solution)/shard_map/products/pallas_call | solution.py:172
  72.6 5.5 %all-to-all-start.1 = ((bf16[128,64,128]{2,1,0:T(8,128)(2,1)}), bf16[128,64,128]{2,1,0:T(8,128)(2,1)S(1)}, u32[]{:S(2)}, u32[]{:S(2)}) async-start(bf16[128,64,128]{2,1,0:T(8,128)(2,1)} %bitcast.15), calls=%async_computation.1 | async-start | bytes 4194304 | tf_op jit(solution)/shard_map/all_to_all | solution.py:271
  78.1 0.0 copy-done.2
  78.1 0.0 copy-done.4
  78.1 0.0 copy-done.5
  78.1 0.0 copy-start
  78.1 2.2 %copy-done = f32[64,128,128]{2,1,0:T(8,128)S(1)} copy-done((f32[64,128,128]{2,1,0:T(8,128)S(1)}, f32[64,128,128]{2,1,0:T(8,128)}, u32[]{:S(2)}) %copy-start) | copy-done | bytes 4194328
  80.3 0.0 copy-start.3
  80.3 0.0 copy-start.6
  80.3 0.0 copy-start.7
  80.3 3.2 %gates.1.gating_far = f32[64,128,128]{2,1,0:T(8,128)S(1)} custom-call(f32[64,128,128]{2,1,0:T(8,128)S(1)} %copy-done, f32[1,128]{1,0:T(1,128)S(1)} %bitcast.10, f32[1,128]{1,0:T(1,128)S(1)} %bitcast.12, bf16[128,128]{1,0:T(8,128)(2,1)S(1)} %copy-done.2), custom_call_target="tpu_custom_call" | custom-call | flops 268435456 | bytes 8388608 | tf_op jit(solution)/shard_map/gates/pallas_call | solution.py:125
  83.6 0.0 copy-start.1
  83.6 1.9 %copy-done.1 = f32[64,128,128]{2,1,0:T(8,128)} copy-done((f32[64,128,128]{2,1,0:T(8,128)}, f32[64,128,128]{2,1,0:T(8,128)S(1)}, u32[]{:S(2)}) %copy-start.1) | copy-done | bytes 4194328
  85.5 22.0 %all-to-all-done.1.product = bf16[128,64,128]{2,1,0:T(8,128)(2,1)S(1)} async-done(((bf16[128,64,128]{2,1,0:T(8,128)(2,1)}), bf16[128,64,128]{2,1,0:T(8,128)(2,1)S(1)}, u32[]{:S(2)}, u32[]{:S(2)}) %all-to-all-start.1) | async-done | bytes 2097184 | tf_op jit(solution)/shard_map/all_to_all | solution.py:271
  107.5 0.0 copy-done.3
  107.5 0.0 copy-done.6
  107.5 0.0 copy-done.7
  107.5 5.2 %update.1 = f32[64,128,128]{2,1,0:T(8,128)} custom-call(bf16[128,64,128]{2,1,0:T(8,128)(2,1)S(1)} %all-to-all-done.1.product, f32[64,128,128]{2,1,0:T(8,128)} %copy-done.1, f32[1,128]{1,0:T(1,128)S(1)} %bitcast.13, f32[1,128]{1,0:T(1,128)S(1)} %bitcast.14, bf16[128,128]{1,0:T(8,128)(2,1)S(1)} %copy-done.3), custom_call_target="tpu_custom_call" | custom-call | flops 268435456 | bytes 10485760 | tf_op jit(solution)/shard_map/update/pallas_call | solution.py:240
Async XLA Ops:
  68.9 9.2 %copy-start.2 = (bf16[128,128]{1,0:T(8,128)(2,1)S(1)}, bf16[128,128]{1,0:T(8,128)(2,1)}, u32[]{:S(2)}) copy-start(bf16[128,128]{1,0:T(8,128)(2,1)} %weight.2) | copy-start | bytes 98308
  68.9 9.2 %copy-start.4 = (f32[128]{0:T(128)S(1)}, f32[128]{0:T(128)}, u32[]{:S(2)}) copy-start(f32[128]{0:T(128)} %param.10) | copy-start | bytes 1540
  68.9 9.3 %copy-start.5 = (f32[128]{0:T(128)S(1)}, f32[128]{0:T(128)}, u32[]{:S(2)}) copy-start(f32[128]{0:T(128)} %param.11) | copy-start | bytes 1540
  72.6 35.0 %all-to-all-start.1 = ((bf16[128,64,128]{2,1,0:T(8,128)(2,1)}), bf16[128,64,128]{2,1,0:T(8,128)(2,1)S(1)}, u32[]{:S(2)}, u32[]{:S(2)}) async-start(bf16[128,64,128]{2,1,0:T(8,128)(2,1)} %bitcast.15), calls=%async_computation.1 | async-start | bytes 4194304 | tf_op jit(solution)/shard_map/all_to_all | solution.py:271
  78.1 2.2 %copy-start = (f32[64,128,128]{2,1,0:T(8,128)S(1)}, f32[64,128,128]{2,1,0:T(8,128)}, u32[]{:S(2)}) copy-start(f32[64,128,128]{2,1,0:T(8,128)} %pair.1) | copy-start | bytes 12582916
  80.3 27.2 %copy-start.3 = (bf16[128,128]{1,0:T(8,128)(2,1)S(1)}, bf16[128,128]{1,0:T(8,128)(2,1)}, u32[]{:S(2)}) copy-start(bf16[128,128]{1,0:T(8,128)(2,1)} %weight.3) | copy-start | bytes 98308
  80.3 27.2 %copy-start.6 = (f32[128]{0:T(128)S(1)}, f32[128]{0:T(128)}, u32[]{:S(2)}) copy-start(f32[128]{0:T(128)} %param.16) | copy-start | bytes 1540
  80.3 27.2 %copy-start.7 = (f32[128]{0:T(128)S(1)}, f32[128]{0:T(128)}, u32[]{:S(2)}) copy-start(f32[128]{0:T(128)} %param.17) | copy-start | bytes 1540
  83.6 1.9 %copy-start.1 = (f32[64,128,128]{2,1,0:T(8,128)}, f32[64,128,128]{2,1,0:T(8,128)S(1)}, u32[]{:S(2)}) copy-start(f32[64,128,128]{2,1,0:T(8,128)S(1)} %gates.1.gating_far) | copy-start | bytes 12582916

commit v5 on v4

v5 whole, which is shorter than its diff:
```python
import jax
import jax.numpy as jnp
from jax import lax
from jax.experimental import pallas as pl
from jax.experimental.pallas import tpu as pltpu
from jax.sharding import PartitionSpec as P

F32, BF16 = jnp.float32, jnp.bfloat16
EPS = 1e-05
ROWS = 16
PAD = 4


def in_hbm(*arrays):
    return [pltpu.with_memory_space_constraint(array, pltpu.HBM) for array in arrays]


def sigmoid(values):
    return 0.5 * jnp.tanh(0.5 * values) + 0.5


def edges_kernel(
    pair_far, gain_far, bias_far, left_far, right_far, gate_far, out, gating,
    pair, gain, bias, w_left, w_right, w_gate, weight, left_rows, right_rows, sems,
):
    rows, tokens, channels = pair.shape
    pitch = channels + PAD
    small = [
        pltpu.make_async_copy(far, near, sems.at[place])
        for place, (far, near) in enumerate(
            zip(
                (gain_far, bias_far, left_far, right_far, gate_far),
                (gain, bias, w_left, w_right, w_gate),
            )
        )
    ]

    def fetch(step):
        place = pl.ds(step * ROWS, ROWS)
        return pltpu.make_async_copy(pair_far.at[place], pair.at[place], sems.at[5 + step])

    fetch(0).start()
    for copy in small:
        copy.start()
    for step in range(1, rows // ROWS):
        fetch(step).start()
    for copy in small:
        copy.wait()
    weight[: 2 * channels] = w_left[...].T
    weight[2 * channels :] = w_right[...].T

    gains = jnp.broadcast_to(gain[...], (2 * tokens, channels)).T
    biases = jnp.broadcast_to(bias[...], (2 * tokens, channels)).T

    def body(step, carry):
        fetch(step).wait()
        base = pl.multiple_of(step * ROWS, ROWS)
        for row in range(0, ROWS, 2):
            values = pair[pl.ds(base + row, 2)].reshape(2 * tokens, channels).T
            center = jnp.sum(values, axis=0, keepdims=True) * (1.0 / channels)
            values = values - center
            spread = jnp.sum(values * values, axis=0, keepdims=True) * (1.0 / channels)
            normed = (values * lax.rsqrt(spread + EPS) * gains + biases).astype(BF16)
            projected = jnp.dot(weight[...], normed, preferred_element_type=F32)
            gates = lax.dot_general(
                normed, w_gate[...], (((0,), (0,)), ((), ())), preferred_element_type=F32
            )
            gating[pl.ds(base + row, 2)] = sigmoid(gates).reshape(2, tokens, channels)
            lefts = sigmoid(projected[:channels]) * projected[channels : 2 * channels]
            rights = sigmoid(projected[2 * channels : 3 * channels]) * projected[3 * channels :]
            for half in range(2):
                place = pl.ds((row + half) * pitch, channels)
                lanes = slice(half * tokens, (half + 1) * tokens)
                left_rows[place, :] = lefts[:, lanes]
                right_rows[place, :] = rights[:, lanes]
        for channel in range(channels):
            place = pl.ds(channel, ROWS, stride=pitch)
            out[channel, 0, pl.ds(base, ROWS), :] = left_rows[place, :].astype(BF16)
            out[channel, 1, pl.ds(base, ROWS), :] = right_rows[place, :].astype(BF16)
        return carry

    lax.fori_loop(0, rows // ROWS, body, 0)


def edges(pair, gain, bias, w_left, w_right, w_gate):
    rows, tokens, channels = pair.shape
    far = pl.BlockSpec(memory_space=pltpu.HBM)
    return pl.pallas_call(
        edges_kernel,
        in_specs=[far] * 6,
        out_specs=[pl.BlockSpec(memory_space=pltpu.VMEM)] * 2,
        out_shape=[
            jax.ShapeDtypeStruct((channels, 2, rows, tokens), BF16),
            jax.ShapeDtypeStruct(pair.shape, F32),
        ],
        scratch_shapes=[
            pltpu.VMEM(pair.shape, F32),
            pltpu.VMEM(gain.shape, F32),
            pltpu.VMEM(bias.shape, F32),
            pltpu.VMEM(w_left.shape, BF16),
            pltpu.VMEM(w_right.shape, BF16),
            pltpu.VMEM(w_gate.shape, BF16),
            pltpu.VMEM((4 * channels, channels), BF16),
            pltpu.VMEM((ROWS * (channels + PAD), tokens), F32),
            pltpu.VMEM((ROWS * (channels + PAD), tokens), F32),
            pltpu.SemaphoreType.DMA((5 + rows // ROWS,)),
        ],
        compiler_params=pltpu.CompilerParams(vmem_limit_bytes=20 * 2**20),
        cost_estimate=pl.CostEstimate(
            flops=10 * rows * tokens * channels * channels,
            bytes_accessed=12 * rows * tokens * channels,
            transcendentals=3 * rows * tokens * channels,
        ),
        name="edges",
    )(*in_hbm(pair, gain, bias, w_left, w_right, w_gate))


def product_kernel(both, out, left_turned, right_whole):
    n_rows, n_cols, _, depth, tokens = both.shape
    for col in range(n_cols):
        lanes = slice(col * tokens, (col + 1) * tokens)
        for row in range(n_rows):
            right_whole[row * depth : (row + 1) * depth, lanes] = both[row, col, 1]
        column = jnp.concatenate([both[row, col, 0] for row in range(n_rows)], axis=0)
        left_turned[lanes, :] = column.T
    for col in range(0, n_cols, 2):
        total = jnp.dot(
            left_turned[...],
            right_whole[:, col * tokens : (col + 2) * tokens],
            preferred_element_type=F32,
        ).astype(BF16)
        for part in range(2):
            block = total[:, part * tokens : (part + 1) * tokens]
            out[:, col + part] = block.reshape(n_rows, depth, tokens)


def products(both):
    n_rows, n_cols, _, depth, tokens = both.shape
    size = n_rows * depth
    return pl.pallas_call(
        product_kernel,
        out_shape=jax.ShapeDtypeStruct((n_rows, n_cols, depth, tokens), BF16),
        scratch_shapes=[pltpu.VMEM((size, size), BF16)] * 2,
        compiler_params=pltpu.CompilerParams(vmem_limit_bytes=24 * 2**20),
        cost_estimate=pl.CostEstimate(
            flops=2 * size**3, bytes_accessed=6 * size * size, transcendentals=0
        ),
        name="products",
    )(both)


def update_kernel(
    product, gating, gain, bias, weight, out_far, gains, biases, rows_of, out, sems
):
    channels, rows, tokens = product.shape
    pitch = ROWS + PAD
    steps = rows // ROWS
    def send(step):
        place = pl.ds(step * ROWS, ROWS)
        return pltpu.make_async_copy(out.at[place], out_far.at[place], sems.at[step])

    gains[...] = jnp.broadcast_to(gain[...], (tokens, channels)).T
    biases[...] = jnp.broadcast_to(bias[...], (tokens, channels)).T

    def body(step, carry):
        base = pl.multiple_of(step * ROWS, ROWS)
        load = lambda channel: product[channel, pl.ds(base, ROWS), :].astype(F32)
        center = load(0)
        for channel in range(1, channels):
            center = center + load(channel)
        center = center * (1.0 / channels)
        spread = jnp.zeros_like(center)
        for channel in range(channels):
            offset = load(channel) - center
            spread = spread + offset * offset
        scale = lax.rsqrt(spread * (1.0 / channels) + EPS)
        for channel in range(channels):
            normed = (load(channel) - center) * scale
            normed = normed * gains[channel : channel + 1, :] + biases[channel : channel + 1, :]
            rows_of[pl.ds(channel * pitch, ROWS), :] = normed
        for row in range(ROWS):
            normed = rows_of[pl.ds(row, channels, stride=pitch), :].astype(BF16)
            projected = lax.dot_general(
                normed, weight[...], (((0,), (0,)), ((), ())), preferred_element_type=F32
            )
            out[base + row] = gating[base + row] * projected
        send(step).start()
        return carry

    lax.fori_loop(0, steps, body, 0)
    for step in range(steps):
        send(step).wait()


def update(product, gating, gain, bias, weight):
    channels, rows, tokens = product.shape
    return pl.pallas_call(
        update_kernel,
        in_specs=[pl.BlockSpec(memory_space=pltpu.VMEM)] * 5,
        out_specs=pl.BlockSpec(memory_space=pltpu.HBM),
        out_shape=jax.ShapeDtypeStruct((rows, tokens, channels), F32),
        scratch_shapes=[
            pltpu.VMEM((channels, tokens), F32),
            pltpu.VMEM((channels, tokens), F32),
            pltpu.VMEM((channels * (ROWS + PAD), tokens), F32),
            pltpu.VMEM((rows, tokens, channels), F32),
            pltpu.SemaphoreType.DMA((rows // ROWS,)),
        ],
        compiler_params=pltpu.CompilerParams(vmem_limit_bytes=20 * 2**20),
        cost_estimate=pl.CostEstimate(
            flops=2 * rows * tokens * channels * channels,
            bytes_accessed=10 * rows * tokens * channels,
            transcendentals=0,
        ),
        name="update",
    )(product, gating, gain, bias, weight)


def per_device(n_rows, n_cols, pair, ln_gain, ln_bias, w_left, w_right, w_gate, w_out, out_gain, out_bias):
    rows, tokens, channels = pair.shape
    axes = ("row", "col")
    gain, bias = ln_gain[None], ln_bias[None]
    both, gating = edges(pair, gain, bias, w_left, w_right, w_gate)
    both = lax.all_to_all(both.reshape(channels, 2 * rows, tokens), axes, 0, 0, tiled=True)
    product = products(both.reshape(n_rows, n_cols, 2, rows, tokens)).reshape(channels, rows, tokens)
    product = lax.all_to_all(product, axes, 0, 0, tiled=True)
    return update(product, gating, out_gain[None], out_bias[None], w_out)


def solution(mesh):
    n_rows, n_cols = mesh.shape["row"], mesh.shape["col"]
    return jax.shard_map(
        lambda *args: per_device(n_rows, n_cols, *args),
        mesh=mesh,
        in_specs=(P("row", "col", None), P(), P(), P(), P(), P(), P(), P(), P()),
        out_specs=P("row", "col", None),
        check_vma=False,
    )
```

time: 113 us -> 112 us (level)
  blocking collectives: 63.1 us -> 97.9 us
  waiting for transfers between devices: 22 us -> 0 us
  starting transfers between devices: 5.53 us -> 0 us
  local copies, waits for them, and re-layouts: 4.15 us -> 0.01 us
  Pallas kernels: 17.9 us -> 13.8 us
    all_to_all x1 -> x2, blocking collectives: 63.1 us -> 97.9 us  [the longest x1 63.1 us: per_device(): lax.all_to_all(both.reshape(channels, 2 * rows, tokens), axes, 0, 0, tile...]
    all_to_all x1 -> x0, waiting for transfers between devices: 22 us -> none  [per_device(): product = lax.all_to_all(product, axes, 0, 0, tiled=True)]
    all_to_all x1 -> x0, starting transfers between devices: 5.53 us -> none  [per_device(): product = lax.all_to_all(product, axes, 0, 0, tiled=True)]
    unnamed x16 -> x6, local copies, waits for them, and re-layouts: 4.15 us -> 0.01 us
    pallas_call x4 -> x3, Pallas kernels: 17.9 us -> 13.8 us  [the longest x1 6.44 us: edges(): pl.pallas_call(edges_kernel, in_specs=[far] * 6, out_specs=[pl.BlockSpec(...]
  transfers between devices with their start and end apart: 1 -> 0, of which waited for: 1 -> 0; matrix products, arithmetic and copies ran while one was open for 0% -> 0% of each run, Pallas kernels for 3% -> 0%
where the time goes in v5:
time: 112 us
  blocking collectives  97.9 us (87%)
  Pallas kernels  13.8 us (12%)
    all_to_all x1, blocking collectives, per_device(): lax.all_to_all(both.reshape(channels, 2 * rows, tokens), axes, 0, 0, tile...  63.1 us
    all_to_all x1, blocking collectives, per_device(): product = lax.all_to_all(product, axes, 0, 0, tiled=True)  34.8 us
    pallas_call x1, Pallas kernels, edges(): pl.pallas_call(edges_kernel, in_specs=[far] * 6, out_specs=[pl.BlockSpec(...  6.44 us
    pallas_call x1, Pallas kernels, update(): pl.pallas_call(update_kernel, in_specs=[pl.BlockSpec(memory_space=pltpu.V...  4.75 us
    pallas_call x1, Pallas kernels, products(): pl.pallas_call(product_kernel, out_shape=jax.ShapeDtypeStruct((n_rows, n_...  2.57 us

profile of v5, /device:TPU:0, one launch (start us, length us, event | category | flops | bytes accessed | tf_op | source)
XLA Modules:
  0.0 111.7 jit_solution(8855479047288998821)
XLA Ops:
  0.0 6.4 %edges.1 = (bf16[128,2,64,128]{3,2,1,0:T(8,128)(2,1)S(1)}, f32[64,128,128]{2,1,0:T(8,128)S(1)}) custom-call(f32[64,128,128]{2,1,0:T(8,128)} %pair_far.1, f32[1,128]{1,0:T(1,128)} %bitcast.12, f32[1,128]{1,0:T(1,128)} %bitcast.13, bf16[128,256]{1,0:T(8,128)(2,1)} %left_far.1, bf16[128,256]{1,0:T(8,128)(2,1)} %right_far.1, bf16[128,128]{1,0:T(8,128)(2,1)} %gate_far.1), custom_call_target="tpu_custom_call" | custom-call | flops 1342177280 | bytes 12582912 | tf_op jit(solution)/shard_map/edges/pallas_call | solution.py:88
  6.4 63.1 %all_to_all.10 = bf16[128,128,128]{2,1,0:T(8,128)(2,1)S(1)} all-to-all(bf16[128,128,128]{2,1,0:T(8,128)(2,1)S(1)} %bitcast.7), channel_id=1, replica_groups=mesh['row'=16,'col'=8] {'row','col'}, dimensions={0} | all-to-all | bytes 8388608 | tf_op jit(solution)/shard_map/all_to_all | solution.py:224
  69.6 0.0 copy-start
  69.6 0.0 copy-start.1
  69.6 0.0 copy-start.2
  69.6 2.6 %products.1 = bf16[16,8,64,128]{3,2,1,0:T(8,128)(2,1)S(1)} custom-call(bf16[16,8,2,64,128]{4,3,2,1,0:T(8,128)(2,1)S(1)} %bitcast.8), custom_call_target="tpu_custom_call" | custom-call | flops 2147483648 | bytes 6291456 | tf_op jit(solution)/shard_map/products/pallas_call | solution.py:140
  72.1 34.8 %all_to_all.11.product = bf16[128,64,128]{2,1,0:T(8,128)(2,1)S(1)} all-to-all(bf16[128,64,128]{2,1,0:T(8,128)(2,1)S(1)} %bitcast.9), channel_id=1, replica_groups=mesh['row'=16,'col'=8] {'row','col'}, dimensions={0} | all-to-all | bytes 4194304 | tf_op jit(solution)/shard_map/all_to_all | solution.py:226
  106.9 0.0 copy-done
  106.9 0.0 copy-done.1
  106.9 0.0 copy-done.2
  106.9 4.8 %update.1 = f32[64,128,128]{2,1,0:T(8,128)} custom-call(bf16[128,64,128]{2,1,0:T(8,128)(2,1)S(1)} %all_to_all.11.product, f32[64,128,128]{2,1,0:T(8,128)S(1)} %get-tuple-element.8.gating, f32[1,128]{1,0:T(1,128)S(1)} %bitcast.10, f32[1,128]{1,0:T(1,128)S(1)} %bitcast.11, bf16[128,128]{1,0:T(8,128)(2,1)S(1)} %copy-done), custom_call_target="tpu_custom_call" | custom-call | flops 268435456 | bytes 10485760 | tf_op jit(solution)/shard_map/update/pallas_call | solution.py:197
Async XLA Ops:
  69.6 37.3 %copy-start = (bf16[128,128]{1,0:T(8,128)(2,1)S(1)}, bf16[128,128]{1,0:T(8,128)(2,1)}, u32[]{:S(2)}) copy-start(bf16[128,128]{1,0:T(8,128)(2,1)} %weight.1) | copy-start | bytes 98308
  69.6 37.3 %copy-start.1 = (f32[128]{0:T(128)S(1)}, f32[128]{0:T(128)}, u32[]{:S(2)}) copy-start(f32[128]{0:T(128)} %param.16) | copy-start | bytes 1540
  69.6 37.3 %copy-start.2 = (f32[128]{0:T(128)S(1)}, f32[128]{0:T(128)}, u32[]{:S(2)}) copy-start(f32[128]{0:T(128)} %param.17) | copy-start | bytes 1540

commit v6 on v5

--- a/solution.py
+++ b/solution.py
@@ -8,15 +8,13 @@
 F32, BF16 = jnp.float32, jnp.bfloat16
 EPS = 1e-05
 ROWS = 16
+BATCH = 4
+SEND = 4
 PAD = 4
 
 
 def in_hbm(*arrays):
     return [pltpu.with_memory_space_constraint(array, pltpu.HBM) for array in arrays]
-
-
-def sigmoid(values):
-    return 0.5 * jnp.tanh(0.5 * values) + 0.5
 
 
 def edges_kernel(
@@ -46,17 +44,18 @@
         fetch(step).start()
     for copy in small:
         copy.wait()
-    weight[: 2 * channels] = w_left[...].T
-    weight[2 * channels :] = w_right[...].T
-
-    gains = jnp.broadcast_to(gain[...], (2 * tokens, channels)).T
-    biases = jnp.broadcast_to(bias[...], (2 * tokens, channels)).T
+    weight[: 2 * channels] = w_left[...].T * 0.5
+    weight[2 * channels :] = w_right[...].T * 0.5
+    w_gate[...] = w_gate[...] * 0.5
+
+    gains = jnp.broadcast_to(gain[...], (BATCH * tokens, channels)).T
+    biases = jnp.broadcast_to(bias[...], (BATCH * tokens, channels)).T
 
     def body(step, carry):
         fetch(step).wait()
         base = pl.multiple_of(step * ROWS, ROWS)
-        for row in range(0, ROWS, 2):
-            values = pair[pl.ds(base + row, 2)].reshape(2 * tokens, channels).T
+        for row in range(0, ROWS, BATCH):
+            values = pair[pl.ds(base + row, BATCH)].reshape(BATCH * tokens, channels).T
             center = jnp.sum(values, axis=0, keepdims=True) * (1.0 / channels)
             values = values - center
             spread = jnp.sum(values * values, axis=0, keepdims=True) * (1.0 / channels)
@@ -65,12 +64,13 @@
             gates = lax.dot_general(
                 normed, w_gate[...], (((0,), (0,)), ((), ())), preferred_element_type=F32
             )
-            gating[pl.ds(base + row, 2)] = sigmoid(gates).reshape(2, tokens, channels)
-            lefts = sigmoid(projected[:channels]) * projected[channels : 2 * channels]
-            rights = sigmoid(projected[2 * channels : 3 * channels]) * projected[3 * channels :]
-            for half in range(2):
-                place = pl.ds((row + half) * pitch, channels)
-                lanes = slice(half * tokens, (half + 1) * tokens)
+            gating[pl.ds(base + row, BATCH)] = 0.5 * jnp.tanh(gates).reshape(BATCH, tokens, channels) + 0.5
+            gate_left, left, gate_right, right = jnp.split(projected, 4, axis=0)
+            lefts = (jnp.tanh(gate_left) + 1.0) * left
+            rights = (jnp.tanh(gate_right) + 1.0) * right
+            for part in range(BATCH):
+                place = pl.ds((row + part) * pitch, channels)
+                lanes = slice(part * tokens, (part + 1) * tokens)
                 left_rows[place, :] = lefts[:, lanes]
                 right_rows[place, :] = rights[:, lanes]
         for channel in range(channels):
@@ -155,9 +155,9 @@
     channels, rows, tokens = product.shape
     pitch = ROWS + PAD
     steps = rows // ROWS
-    def send(step):
-        place = pl.ds(step * ROWS, ROWS)
-        return pltpu.make_async_copy(out.at[place], out_far.at[place], sems.at[step])
+    def send(start):
+        place = pl.ds(start, SEND)
+        return pltpu.make_async_copy(out.at[place], out_far.at[place], sems.at[start // SEND])
 
     gains[...] = jnp.broadcast_to(gain[...], (tokens, channels)).T
     biases[...] = jnp.broadcast_to(bias[...], (tokens, channels)).T
@@ -165,15 +165,16 @@
     def body(step, carry):
         base = pl.multiple_of(step * ROWS, ROWS)
         load = lambda channel: product[channel, pl.ds(base, ROWS), :].astype(F32)
-        center = load(0)
+        first = load(0)
+        total = jnp.zeros_like(first)
+        spread = jnp.zeros_like(first)
         for channel in range(1, channels):
-            center = center + load(channel)
-        center = center * (1.0 / channels)
-        spread = jnp.zeros_like(center)
-        for channel in range(channels):
-            offset = load(channel) - center
+            offset = load(channel) - first
+            total = total + offset
             spread = spread + offset * offset
-        scale = lax.rsqrt(spread * (1.0 / channels) + EPS)
+        total = total * (1.0 / channels)
+        center = first + total
+        scale = lax.rsqrt(spread * (1.0 / channels) - total * total + EPS)
         for channel in range(channels):
             normed = (load(channel) - center) * scale
             normed = normed * gains[channel : channel + 1, :] + biases[channel : channel + 1, :]
@@ -184,12 +185,13 @@
                 normed, weight[...], (((0,), (0,)), ((), ())), preferred_element_type=F32
             )
             out[base + row] = gating[base + row] * projected
-        send(step).start()
+            if row % SEND == SEND - 1:
+                send(base + row + 1 - SEND).start()
         return carry
 
     lax.fori_loop(0, steps, body, 0)
-    for step in range(steps):
-        send(step).wait()
+    for start in range(0, rows, SEND):
+        send(start).wait()
 
 
 def update(product, gating, gain, bias, weight):
@@ -204,7 +206,7 @@
             pltpu.VMEM((channels, tokens), F32),
             pltpu.VMEM((channels * (ROWS + PAD), tokens), F32),
             pltpu.VMEM((rows, tokens, channels), F32),
-            pltpu.SemaphoreType.DMA((rows // ROWS,)),
+            pltpu.SemaphoreType.DMA((rows // SEND,)),
         ],
         compiler_params=pltpu.CompilerParams(vmem_limit_bytes=20 * 2**20),
         cost_estimate=pl.CostEstimate(

time: 112 us -> 111 us (level)
  no operation moved by 1% of the time
where the time goes in v6:
time: 111 us
  blocking collectives  97.9 us (88%)
  Pallas kernels  12.9 us (12%)
    all_to_all x1, blocking collectives, per_device(): lax.all_to_all(both.reshape(channels, 2 * rows, tokens), axes, 0, 0, tile...  63.1 us
    all_to_all x1, blocking collectives, per_device(): product = lax.all_to_all(product, axes, 0, 0, tiled=True)  34.8 us
    pallas_call x1, Pallas kernels, edges(): pl.pallas_call(edges_kernel, in_specs=[far] * 6, out_specs=[pl.BlockSpec(...  6.14 us
    pallas_call x1, Pallas kernels, update(): pl.pallas_call(update_kernel, in_specs=[pl.BlockSpec(memory_space=pltpu.V...  4.18 us
    pallas_call x1, Pallas kernels, products(): pl.pallas_call(product_kernel, out_shape=jax.ShapeDtypeStruct((n_rows, n_...  2.56 us

profile of v6, /device:TPU:0, one launch (start us, length us, event | category | flops | bytes accessed | tf_op | source)
XLA Modules:
  0.0 110.8 jit_solution(17421255095113961468)
XLA Ops:
  0.0 6.1 %edges.1 = (bf16[128,2,64,128]{3,2,1,0:T(8,128)(2,1)S(1)}, f32[64,128,128]{2,1,0:T(8,128)S(1)}) custom-call(f32[64,128,128]{2,1,0:T(8,128)} %pair_far.1, f32[1,128]{1,0:T(1,128)} %bitcast.12, f32[1,128]{1,0:T(1,128)} %bitcast.13, bf16[128,256]{1,0:T(8,128)(2,1)} %left_far.1, bf16[128,256]{1,0:T(8,128)(2,1)} %right_far.1, bf16[128,128]{1,0:T(8,128)(2,1)} %gate_far.1), custom_call_target="tpu_custom_call" | custom-call | flops 1342177280 | bytes 12582912 | tf_op jit(solution)/shard_map/edges/pallas_call | solution.py:88
  6.2 63.1 %all_to_all.10 = bf16[128,128,128]{2,1,0:T(8,128)(2,1)S(1)} all-to-all(bf16[128,128,128]{2,1,0:T(8,128)(2,1)S(1)} %bitcast.7), channel_id=1, replica_groups=mesh['row'=16,'col'=8] {'row','col'}, dimensions={0} | all-to-all | bytes 8388608 | tf_op jit(solution)/shard_map/all_to_all | solution.py:226
  69.3 0.0 copy-start
  69.3 0.0 copy-start.1
  69.3 0.0 copy-start.2
  69.3 2.6 %products.1 = bf16[16,8,64,128]{3,2,1,0:T(8,128)(2,1)S(1)} custom-call(bf16[16,8,2,64,128]{4,3,2,1,0:T(8,128)(2,1)S(1)} %bitcast.8), custom_call_target="tpu_custom_call" | custom-call | flops 2147483648 | bytes 6291456 | tf_op jit(solution)/shard_map/products/pallas_call | solution.py:140
  71.8 34.8 %all_to_all.11.product = bf16[128,64,128]{2,1,0:T(8,128)(2,1)S(1)} all-to-all(bf16[128,64,128]{2,1,0:T(8,128)(2,1)S(1)} %bitcast.9), channel_id=1, replica_groups=mesh['row'=16,'col'=8] {'row','col'}, dimensions={0} | all-to-all | bytes 4194304 | tf_op jit(solution)/shard_map/all_to_all | solution.py:228
  106.6 0.0 copy-done
  106.6 0.0 copy-done.1
  106.6 0.0 copy-done.2
  106.6 4.2 %update.1 = f32[64,128,128]{2,1,0:T(8,128)} custom-call(bf16[128,64,128]{2,1,0:T(8,128)(2,1)S(1)} %all_to_all.11.product, f32[64,128,128]{2,1,0:T(8,128)S(1)} %get-tuple-element.8.gating, f32[1,128]{1,0:T(1,128)S(1)} %bitcast.10, f32[1,128]{1,0:T(1,128)S(1)} %bitcast.11, bf16[128,128]{1,0:T(8,128)(2,1)S(1)} %copy-done), custom_call_target="tpu_custom_call" | custom-call | flops 268435456 | bytes 10485760 | tf_op jit(solution)/shard_map/update/pallas_call | solution.py:199
Async XLA Ops:
  69.3 37.3 %copy-start = (bf16[128,128]{1,0:T(8,128)(2,1)S(1)}, bf16[128,128]{1,0:T(8,128)(2,1)}, u32[]{:S(2)}) copy-start(bf16[128,128]{1,0:T(8,128)(2,1)} %weight.1) | copy-start | bytes 98308
  69.3 37.3 %copy-start.1 = (f32[128]{0:T(128)S(1)}, f32[128]{0:T(128)}, u32[]{:S(2)}) copy-start(f32[128]{0:T(128)} %param.16) | copy-start | bytes 1540
  69.3 37.3 %copy-start.2 = (f32[128]{0:T(128)S(1)}, f32[128]{0:T(128)}, u32[]{:S(2)}) copy-start(f32[128]{0:T(128)} %param.17) | copy-start | bytes 1540

commit v7 on v6

--- a/solution.py
+++ b/solution.py
@@ -164,23 +164,16 @@
 
     def body(step, carry):
         base = pl.multiple_of(step * ROWS, ROWS)
-        load = lambda channel: product[channel, pl.ds(base, ROWS), :].astype(F32)
-        first = load(0)
-        total = jnp.zeros_like(first)
-        spread = jnp.zeros_like(first)
-        for channel in range(1, channels):
-            offset = load(channel) - first
-            total = total + offset
-            spread = spread + offset * offset
-        total = total * (1.0 / channels)
-        center = first + total
-        scale = lax.rsqrt(spread * (1.0 / channels) - total * total + EPS)
         for channel in range(channels):
-            normed = (load(channel) - center) * scale
-            normed = normed * gains[channel : channel + 1, :] + biases[channel : channel + 1, :]
-            rows_of[pl.ds(channel * pitch, ROWS), :] = normed
+            rows_of[pl.ds(channel * pitch, ROWS), :] = product[
+                channel, pl.ds(base, ROWS), :
+            ].astype(F32)
         for row in range(ROWS):
-            normed = rows_of[pl.ds(row, channels, stride=pitch), :].astype(BF16)
+            values = rows_of[pl.ds(row, channels, stride=pitch), :]
+            center = jnp.sum(values, axis=0, keepdims=True) * (1.0 / channels)
+            values = values - center
+            spread = jnp.sum(values * values, axis=0, keepdims=True) * (1.0 / channels)
+            normed = (values * lax.rsqrt(spread + EPS) * gains[...] + biases[...]).astype(BF16)
             projected = lax.dot_general(
                 normed, weight[...], (((0,), (0,)), ((), ())), preferred_element_type=F32
             )

time: 111 us -> 111 us (level)
  no operation moved by 1% of the time
where the time goes in v7:
time: 111 us; the launch traced here: 110 us
  blocking collectives  97.9 us (88%)
  Pallas kernels  12.5 us (11%)
    all_to_all x1, blocking collectives, per_device(): lax.all_to_all(both.reshape(channels, 2 * rows, tokens), axes, 0, 0, tile...  63.1 us
    all_to_all x1, blocking collectives, per_device(): product = lax.all_to_all(product, axes, 0, 0, tiled=True)  34.8 us
    pallas_call x1, Pallas kernels, edges(): pl.pallas_call(edges_kernel, in_specs=[far] * 6, out_specs=[pl.BlockSpec(...  6.14 us
    pallas_call x1, Pallas kernels, update(): pl.pallas_call(update_kernel, in_specs=[pl.BlockSpec(memory_space=pltpu.V...  3.79 us
    pallas_call x1, Pallas kernels, products(): pl.pallas_call(product_kernel, out_shape=jax.ShapeDtypeStruct((n_rows, n_...  2.56 us

profile of v7, /device:TPU:0, one launch (start us, length us, event | category | flops | bytes accessed | tf_op | source)
XLA Modules:
  0.0 110.4 jit_solution(15294468093146194941)
XLA Ops:
  0.0 6.1 %edges.1 = (bf16[128,2,64,128]{3,2,1,0:T(8,128)(2,1)S(1)}, f32[64,128,128]{2,1,0:T(8,128)S(1)}) custom-call(f32[64,128,128]{2,1,0:T(8,128)} %pair_far.1, f32[1,128]{1,0:T(1,128)} %bitcast.12, f32[1,128]{1,0:T(1,128)} %bitcast.13, bf16[128,256]{1,0:T(8,128)(2,1)} %left_far.1, bf16[128,256]{1,0:T(8,128)(2,1)} %right_far.1, bf16[128,128]{1,0:T(8,128)(2,1)} %gate_far.1), custom_call_target="tpu_custom_call" | custom-call | flops 1342177280 | bytes 12582912 | tf_op jit(solution)/shard_map/edges/pallas_call | solution.py:88
  6.2 63.1 %all_to_all.10 = bf16[128,128,128]{2,1,0:T(8,128)(2,1)S(1)} all-to-all(bf16[128,128,128]{2,1,0:T(8,128)(2,1)S(1)} %bitcast.7), channel_id=1, replica_groups=mesh['row'=16,'col'=8] {'row','col'}, dimensions={0} | all-to-all | bytes 8388608 | tf_op jit(solution)/shard_map/all_to_all | solution.py:219
  69.3 0.0 copy-start
  69.3 0.0 copy-start.1
  69.3 0.0 copy-start.2
  69.3 2.6 %products.1 = bf16[16,8,64,128]{3,2,1,0:T(8,128)(2,1)S(1)} custom-call(bf16[16,8,2,64,128]{4,3,2,1,0:T(8,128)(2,1)S(1)} %bitcast.8), custom_call_target="tpu_custom_call" | custom-call | flops 2147483648 | bytes 6291456 | tf_op jit(solution)/shard_map/products/pallas_call | solution.py:140
  71.8 34.8 %all_to_all.11.product = bf16[128,64,128]{2,1,0:T(8,128)(2,1)S(1)} all-to-all(bf16[128,64,128]{2,1,0:T(8,128)(2,1)S(1)} %bitcast.9), channel_id=1, replica_groups=mesh['row'=16,'col'=8] {'row','col'}, dimensions={0} | all-to-all | bytes 4194304 | tf_op jit(solution)/shard_map/all_to_all | solution.py:221
  106.6 0.0 copy-done
  106.6 0.0 copy-done.1
  106.6 0.0 copy-done.2
  106.6 3.8 %update.1 = f32[64,128,128]{2,1,0:T(8,128)} custom-call(bf16[128,64,128]{2,1,0:T(8,128)(2,1)S(1)} %all_to_all.11.product, f32[64,128,128]{2,1,0:T(8,128)S(1)} %get-tuple-element.8.gating, f32[1,128]{1,0:T(1,128)S(1)} %bitcast.10, f32[1,128]{1,0:T(1,128)S(1)} %bitcast.11, bf16[128,128]{1,0:T(8,128)(2,1)S(1)} %copy-done), custom_call_target="tpu_custom_call" | custom-call | flops 268435456 | bytes 10485760 | tf_op jit(solution)/shard_map/update/pallas_call | solution.py:192
Async XLA Ops:
  69.3 37.3 %copy-start = (bf16[128,128]{1,0:T(8,128)(2,1)S(1)}, bf16[128,128]{1,0:T(8,128)(2,1)}, u32[]{:S(2)}) copy-start(bf16[128,128]{1,0:T(8,128)(2,1)} %weight.1) | copy-start | bytes 98308
  69.3 37.3 %copy-start.1 = (f32[128]{0:T(128)S(1)}, f32[128]{0:T(128)}, u32[]{:S(2)}) copy-start(f32[128]{0:T(128)} %param.16) | copy-start | bytes 1540
  69.3 37.3 %copy-start.2 = (f32[128]{0:T(128)S(1)}, f32[128]{0:T(128)}, u32[]{:S(2)}) copy-start(f32[128]{0:T(128)} %param.17) | copy-start | bytes 1540

commit v8 on v7

--- a/solution.py
+++ b/solution.py
@@ -7,6 +7,7 @@
 
 F32, BF16 = jnp.float32, jnp.bfloat16
 EPS = 1e-05
+CHUNK = 32
 ROWS = 16
 BATCH = 4
 SEND = 4
@@ -34,13 +35,13 @@
     ]
 
     def fetch(step):
-        place = pl.ds(step * ROWS, ROWS)
+        place = pl.ds(step * CHUNK, CHUNK)
         return pltpu.make_async_copy(pair_far.at[place], pair.at[place], sems.at[5 + step])
 
     fetch(0).start()
     for copy in small:
         copy.start()
-    for step in range(1, rows // ROWS):
+    for step in range(1, rows // CHUNK):
         fetch(step).start()
     for copy in small:
         copy.wait()
@@ -53,8 +54,8 @@
 
     def body(step, carry):
         fetch(step).wait()
-        base = pl.multiple_of(step * ROWS, ROWS)
-        for row in range(0, ROWS, BATCH):
+        base = pl.multiple_of(step * CHUNK, CHUNK)
+        for row in range(0, CHUNK, BATCH):
             values = pair[pl.ds(base + row, BATCH)].reshape(BATCH * tokens, channels).T
             center = jnp.sum(values, axis=0, keepdims=True) * (1.0 / channels)
             values = values - center
@@ -74,12 +75,12 @@
                 left_rows[place, :] = lefts[:, lanes]
                 right_rows[place, :] = rights[:, lanes]
         for channel in range(channels):
-            place = pl.ds(channel, ROWS, stride=pitch)
-            out[channel, 0, pl.ds(base, ROWS), :] = left_rows[place, :].astype(BF16)
-            out[channel, 1, pl.ds(base, ROWS), :] = right_rows[place, :].astype(BF16)
+            place = pl.ds(channel, CHUNK, stride=pitch)
+            out[channel, 0, pl.ds(base, CHUNK), :] = left_rows[place, :].astype(BF16)
+            out[channel, 1, pl.ds(base, CHUNK), :] = right_rows[place, :].astype(BF16)
         return carry
 
-    lax.fori_loop(0, rows // ROWS, body, 0)
+    lax.fori_loop(0, rows // CHUNK, body, 0)
 
 
 def edges(pair, gain, bias, w_left, w_right, w_gate):
@@ -101,9 +102,9 @@
             pltpu.VMEM(w_right.shape, BF16),
             pltpu.VMEM(w_gate.shape, BF16),
             pltpu.VMEM((4 * channels, channels), BF16),
-            pltpu.VMEM((ROWS * (channels + PAD), tokens), F32),
-            pltpu.VMEM((ROWS * (channels + PAD), tokens), F32),
-            pltpu.SemaphoreType.DMA((5 + rows // ROWS,)),
+            pltpu.VMEM((CHUNK * (channels + PAD), tokens), F32),
+            pltpu.VMEM((CHUNK * (channels + PAD), tokens), F32),
+            pltpu.SemaphoreType.DMA((5 + rows // CHUNK,)),
         ],
         compiler_params=pltpu.CompilerParams(vmem_limit_bytes=20 * 2**20),
         cost_estimate=pl.CostEstimate(
@@ -115,20 +116,17 @@
     )(*in_hbm(pair, gain, bias, w_left, w_right, w_gate))
 
 
-def product_kernel(both, out, left_turned, right_whole):
+def product_kernel(both, out, left_turned):
     n_rows, n_cols, _, depth, tokens = both.shape
+
+    def column(col, side):
+        return jnp.concatenate([both[row, col, side] for row in range(n_rows)], axis=0)
+
     for col in range(n_cols):
-        lanes = slice(col * tokens, (col + 1) * tokens)
-        for row in range(n_rows):
-            right_whole[row * depth : (row + 1) * depth, lanes] = both[row, col, 1]
-        column = jnp.concatenate([both[row, col, 0] for row in range(n_rows)], axis=0)
-        left_turned[lanes, :] = column.T
+        left_turned[col * tokens : (col + 1) * tokens, :] = column(col, 0).T
     for col in range(0, n_cols, 2):
-        total = jnp.dot(
-            left_turned[...],
-            right_whole[:, col * tokens : (col + 2) * tokens],
-            preferred_element_type=F32,
-        ).astype(BF16)
+        rights = jnp.concatenate([column(col, 1), column(col + 1, 1)], axis=1)
+        total = jnp.dot(left_turned[...], rights, preferred_element_type=F32).astype(BF16)
         for part in range(2):
             block = total[:, part * tokens : (part + 1) * tokens]
             out[:, col + part] = block.reshape(n_rows, depth, tokens)
@@ -140,7 +138,7 @@
     return pl.pallas_call(
         product_kernel,
         out_shape=jax.ShapeDtypeStruct((n_rows, n_cols, depth, tokens), BF16),
-        scratch_shapes=[pltpu.VMEM((size, size), BF16)] * 2,
+        scratch_shapes=[pltpu.VMEM((size, size), BF16)],
         compiler_params=pltpu.CompilerParams(vmem_limit_bytes=24 * 2**20),
         cost_estimate=pl.CostEstimate(
             flops=2 * size**3, bytes_accessed=6 * size * size, transcendentals=0
@@ -182,7 +180,7 @@
                 send(base + row + 1 - SEND).start()
         return carry
 
-    lax.fori_loop(0, steps, body, 0)
+    lax.fori_loop(0, steps, body, 0, unroll=True)
     for start in range(0, rows, SEND):
         send(start).wait()
 

time: 111 us -> 110 us (level)
  no operation moved by 1% of the time
where the time goes in v8:
time: 110 us
  blocking collectives  97.9 us (89%)
  Pallas kernels  11.7 us (11%)
    all_to_all x1, blocking collectives, per_device(): lax.all_to_all(both.reshape(channels, 2 * rows, tokens), axes, 0, 0, tile...  63.1 us
    all_to_all x1, blocking collectives, per_device(): product = lax.all_to_all(product, axes, 0, 0, tiled=True)  34.8 us
    pallas_call x1, Pallas kernels, edges(): pl.pallas_call(edges_kernel, in_specs=[far] * 6, out_specs=[pl.BlockSpec(...  5.96 us
    pallas_call x1, Pallas kernels, update(): pl.pallas_call(update_kernel, in_specs=[pl.BlockSpec(memory_space=pltpu.V...  3.36 us
    pallas_call x1, Pallas kernels, products(): pl.pallas_call(product_kernel, out_shape=jax.ShapeDtypeStruct((n_rows, n_...  2.36 us

profile of v8, /device:TPU:0, one launch (start us, length us, event | category | flops | bytes accessed | tf_op | source)
XLA Modules:
  0.0 109.6 jit_solution(7738952375426147585)
XLA Ops:
  0.0 6.0 %edges.1 = (bf16[128,2,64,128]{3,2,1,0:T(8,128)(2,1)S(1)}, f32[64,128,128]{2,1,0:T(8,128)S(1)}) custom-call(f32[64,128,128]{2,1,0:T(8,128)} %pair_far.1, f32[1,128]{1,0:T(1,128)} %bitcast.12, f32[1,128]{1,0:T(1,128)} %bitcast.13, bf16[128,256]{1,0:T(8,128)(2,1)} %left_far.1, bf16[128,256]{1,0:T(8,128)(2,1)} %right_far.1, bf16[128,128]{1,0:T(8,128)(2,1)} %gate_far.1), custom_call_target="tpu_custom_call" | custom-call | flops 1342177280 | bytes 12582912 | tf_op jit(solution)/shard_map/edges/pallas_call | solution.py:89
  6.0 63.1 %all_to_all.10 = bf16[128,128,128]{2,1,0:T(8,128)(2,1)S(1)} all-to-all(bf16[128,128,128]{2,1,0:T(8,128)(2,1)S(1)} %bitcast.7), channel_id=1, replica_groups=mesh['row'=16,'col'=8] {'row','col'}, dimensions={0} | all-to-all | bytes 8388608 | tf_op jit(solution)/shard_map/all_to_all | solution.py:217
  69.1 0.0 copy-start
  69.1 0.0 copy-start.1
  69.1 0.0 copy-start.2
  69.1 2.4 %products.1 = bf16[16,8,64,128]{3,2,1,0:T(8,128)(2,1)S(1)} custom-call(bf16[16,8,2,64,128]{4,3,2,1,0:T(8,128)(2,1)S(1)} %bitcast.8), custom_call_target="tpu_custom_call" | custom-call | flops 2147483648 | bytes 6291456 | tf_op jit(solution)/shard_map/products/pallas_call | solution.py:138
  71.4 34.8 %all_to_all.11.product = bf16[128,64,128]{2,1,0:T(8,128)(2,1)S(1)} all-to-all(bf16[128,64,128]{2,1,0:T(8,128)(2,1)S(1)} %bitcast.9), channel_id=1, replica_groups=mesh['row'=16,'col'=8] {'row','col'}, dimensions={0} | all-to-all | bytes 4194304 | tf_op jit(solution)/shard_map/all_to_all | solution.py:219
  106.2 0.0 copy-done
  106.2 0.0 copy-done.1
  106.2 0.0 copy-done.2
  106.2 3.4 %update.1 = f32[64,128,128]{2,1,0:T(8,128)} custom-call(bf16[128,64,128]{2,1,0:T(8,128)(2,1)S(1)} %all_to_all.11.product, f32[64,128,128]{2,1,0:T(8,128)S(1)} %get-tuple-element.8.gating, f32[1,128]{1,0:T(1,128)S(1)} %bitcast.10, f32[1,128]{1,0:T(1,128)S(1)} %bitcast.11, bf16[128,128]{1,0:T(8,128)(2,1)S(1)} %copy-done), custom_call_target="tpu_custom_call" | custom-call | flops 268435456 | bytes 10485760 | tf_op jit(solution)/shard_map/update/pallas_call | solution.py:190
Async XLA Ops:
  69.1 37.1 %copy-start = (bf16[128,128]{1,0:T(8,128)(2,1)S(1)}, bf16[128,128]{1,0:T(8,128)(2,1)}, u32[]{:S(2)}) copy-start(bf16[128,128]{1,0:T(8,128)(2,1)} %weight.1) | copy-start | bytes 98308
  69.1 37.1 %copy-start.1 = (f32[128]{0:T(128)S(1)}, f32[128]{0:T(128)}, u32[]{:S(2)}) copy-start(f32[128]{0:T(128)} %param.16) | copy-start | bytes 1540
  69.1 37.1 %copy-start.2 = (f32[128]{0:T(128)S(1)}, f32[128]{0:T(128)}, u32[]{:S(2)}) copy-start(f32[128]{0:T(128)} %param.17) | copy-start | bytes 1540

commit v9 on v8

--- a/solution.py
+++ b/solution.py
@@ -7,7 +7,7 @@
 
 F32, BF16 = jnp.float32, jnp.bfloat16
 EPS = 1e-05
-CHUNK = 32
+FIRST = 16
 ROWS = 16
 BATCH = 4
 SEND = 4
@@ -34,15 +34,19 @@
         )
     ]
 
-    def fetch(step):
-        place = pl.ds(step * CHUNK, CHUNK)
-        return pltpu.make_async_copy(pair_far.at[place], pair.at[place], sems.at[5 + step])
-
-    fetch(0).start()
+    steps = [(0, FIRST), (FIRST, rows)]
+    fetches = [
+        pltpu.make_async_copy(
+            pair_far.at[pl.ds(start, stop - start)],
+            pair.at[pl.ds(start, stop - start)],
+            sems.at[5 + step],
+        )
+        for step, (start, stop) in enumerate(steps)
+    ]
+    fetches[0].start()
     for copy in small:
         copy.start()
-    for step in range(1, rows // CHUNK):
-        fetch(step).start()
+    fetches[1].start()
     for copy in small:
         copy.wait()
     weight[: 2 * channels] = w_left[...].T * 0.5
@@ -52,11 +56,10 @@
     gains = jnp.broadcast_to(gain[...], (BATCH * tokens, channels)).T
     biases = jnp.broadcast_to(bias[...], (BATCH * tokens, channels)).T
 
-    def body(step, carry):
-        fetch(step).wait()
-        base = pl.multiple_of(step * CHUNK, CHUNK)
-        for row in range(0, CHUNK, BATCH):
-            values = pair[pl.ds(base + row, BATCH)].reshape(BATCH * tokens, channels).T
+    for copy, (start, stop) in zip(fetches, steps):
+        copy.wait()
+        for row in range(start, stop, BATCH):
+            values = pair[pl.ds(row, BATCH)].reshape(BATCH * tokens, channels).T
             center = jnp.sum(values, axis=0, keepdims=True) * (1.0 / channels)
             values = values - center
             spread = jnp.sum(values * values, axis=0, keepdims=True) * (1.0 / channels)
@@ -65,7 +68,7 @@
             gates = lax.dot_general(
                 normed, w_gate[...], (((0,), (0,)), ((), ())), preferred_element_type=F32
             )
-            gating[pl.ds(base + row, BATCH)] = 0.5 * jnp.tanh(gates).reshape(BATCH, tokens, channels) + 0.5
+            gating[pl.ds(row, BATCH)] = 0.5 * jnp.tanh(gates).reshape(BATCH, tokens, channels) + 0.5
             gate_left, left, gate_right, right = jnp.split(projected, 4, axis=0)
             lefts = (jnp.tanh(gate_left) + 1.0) * left
             rights = (jnp.tanh(gate_right) + 1.0) * right
@@ -75,12 +78,9 @@
                 left_rows[place, :] = lefts[:, lanes]
                 right_rows[place, :] = rights[:, lanes]
         for channel in range(channels):
-            place = pl.ds(channel, CHUNK, stride=pitch)
-            out[channel, 0, pl.ds(base, CHUNK), :] = left_rows[place, :].astype(BF16)
-            out[channel, 1, pl.ds(base, CHUNK), :] = right_rows[place, :].astype(BF16)
-        return carry
-
-    lax.fori_loop(0, rows // CHUNK, body, 0)
+            place = pl.ds(start * pitch + channel, stop - start, stride=pitch)
+            out[channel, 0, start:stop, :] = left_rows[place, :].astype(BF16)
+            out[channel, 1, start:stop, :] = right_rows[place, :].astype(BF16)
 
 
 def edges(pair, gain, bias, w_left, w_right, w_gate):
@@ -102,11 +102,11 @@
             pltpu.VMEM(w_right.shape, BF16),
             pltpu.VMEM(w_gate.shape, BF16),
             pltpu.VMEM((4 * channels, channels), BF16),
-            pltpu.VMEM((CHUNK * (channels + PAD), tokens), F32),
-            pltpu.VMEM((CHUNK * (channels + PAD), tokens), F32),
-            pltpu.SemaphoreType.DMA((5 + rows // CHUNK,)),
+            pltpu.VMEM((rows * (channels + PAD), tokens), F32),
+            pltpu.VMEM((rows * (channels + PAD), tokens), F32),
+            pltpu.SemaphoreType.DMA((7,)),
         ],
-        compiler_params=pltpu.CompilerParams(vmem_limit_bytes=20 * 2**20),
+        compiler_params=pltpu.CompilerParams(vmem_limit_bytes=28 * 2**20),
         cost_estimate=pl.CostEstimate(
             flops=10 * rows * tokens * channels * channels,
             bytes_accessed=12 * rows * tokens * channels,

time: 110 us -> 109 us (level)
  no operation moved by 1% of the time
where the time goes in v9:
time: 109 us
  blocking collectives  97.9 us (90%)
  Pallas kernels  11.3 us (10%)
    all_to_all x1, blocking collectives, per_device(): lax.all_to_all(both.reshape(channels, 2 * rows, tokens), axes, 0, 0, tile...  63.1 us
    all_to_all x1, blocking collectives, per_device(): product = lax.all_to_all(product, axes, 0, 0, tiled=True)  34.8 us
    pallas_call x1, Pallas kernels, edges(): pl.pallas_call(edges_kernel, in_specs=[far] * 6, out_specs=[pl.BlockSpec(...  5.59 us
    pallas_call x1, Pallas kernels, update(): pl.pallas_call(update_kernel, in_specs=[pl.BlockSpec(memory_space=pltpu.V...  3.36 us
    pallas_call x1, Pallas kernels, products(): pl.pallas_call(product_kernel, out_shape=jax.ShapeDtypeStruct((n_rows, n_...  2.36 us

profile of v9, /device:TPU:0, one launch (start us, length us, event | category | flops | bytes accessed | tf_op | source)
XLA Modules:
  0.0 109.2 jit_solution(9723380341755137888)
XLA Ops:
  0.0 5.6 %edges.1 = (bf16[128,2,64,128]{3,2,1,0:T(8,128)(2,1)S(1)}, f32[64,128,128]{2,1,0:T(8,128)S(1)}) custom-call(f32[64,128,128]{2,1,0:T(8,128)} %pair_far.1, f32[1,128]{1,0:T(1,128)} %bitcast.12, f32[1,128]{1,0:T(1,128)} %bitcast.13, bf16[128,256]{1,0:T(8,128)(2,1)} %left_far.1, bf16[128,256]{1,0:T(8,128)(2,1)} %right_far.1, bf16[128,128]{1,0:T(8,128)(2,1)} %gate_far.1), custom_call_target="tpu_custom_call" | custom-call | flops 1342177280 | bytes 12582912 | tf_op jit(solution)/shard_map/edges/pallas_call | solution.py:89
  5.6 63.1 %all_to_all.10 = bf16[128,128,128]{2,1,0:T(8,128)(2,1)S(1)} all-to-all(bf16[128,128,128]{2,1,0:T(8,128)(2,1)S(1)} %bitcast.7), channel_id=1, replica_groups=mesh['row'=16,'col'=8] {'row','col'}, dimensions={0} | all-to-all | bytes 8388608 | tf_op jit(solution)/shard_map/all_to_all | solution.py:217
  68.7 0.0 copy-start
  68.7 0.0 copy-start.1
  68.7 0.0 copy-start.2
  68.7 2.4 %products.1 = bf16[16,8,64,128]{3,2,1,0:T(8,128)(2,1)S(1)} custom-call(bf16[16,8,2,64,128]{4,3,2,1,0:T(8,128)(2,1)S(1)} %bitcast.8), custom_call_target="tpu_custom_call" | custom-call | flops 2147483648 | bytes 6291456 | tf_op jit(solution)/shard_map/products/pallas_call | solution.py:138
  71.1 34.8 %all_to_all.11.product = bf16[128,64,128]{2,1,0:T(8,128)(2,1)S(1)} all-to-all(bf16[128,64,128]{2,1,0:T(8,128)(2,1)S(1)} %bitcast.9), channel_id=1, replica_groups=mesh['row'=16,'col'=8] {'row','col'}, dimensions={0} | all-to-all | bytes 4194304 | tf_op jit(solution)/shard_map/all_to_all | solution.py:219
  105.8 0.0 copy-done
  105.8 0.0 copy-done.1
  105.8 0.0 copy-done.2
  105.8 3.4 %update.1 = f32[64,128,128]{2,1,0:T(8,128)} custom-call(bf16[128,64,128]{2,1,0:T(8,128)(2,1)S(1)} %all_to_all.11.product, f32[64,128,128]{2,1,0:T(8,128)S(1)} %get-tuple-element.8.gating, f32[1,128]{1,0:T(1,128)S(1)} %bitcast.10, f32[1,128]{1,0:T(1,128)S(1)} %bitcast.11, bf16[128,128]{1,0:T(8,128)(2,1)S(1)} %copy-done), custom_call_target="tpu_custom_call" | custom-call | flops 268435456 | bytes 10485760 | tf_op jit(solution)/shard_map/update/pallas_call | solution.py:190
Async XLA Ops:
  68.7 37.1 %copy-start = (bf16[128,128]{1,0:T(8,128)(2,1)S(1)}, bf16[128,128]{1,0:T(8,128)(2,1)}, u32[]{:S(2)}) copy-start(bf16[128,128]{1,0:T(8,128)(2,1)} %weight.1) | copy-start | bytes 98308
  68.7 37.1 %copy-start.1 = (f32[128]{0:T(128)S(1)}, f32[128]{0:T(128)}, u32[]{:S(2)}) copy-start(f32[128]{0:T(128)} %param.16) | copy-start | bytes 1540
  68.7 37.1 %copy-start.2 = (f32[128]{0:T(128)S(1)}, f32[128]{0:T(128)}, u32[]{:S(2)}) copy-start(f32[128]{0:T(128)} %param.17) | copy-start | bytes 1540

commit v10 on v9

--- a/solution.py
+++ b/solution.py
@@ -19,8 +19,8 @@
 
 
 def edges_kernel(
-    pair_far, gain_far, bias_far, left_far, right_far, gate_far, out, gating,
-    pair, gain, bias, w_left, w_right, w_gate, weight, left_rows, right_rows, sems,
+    pair_far, gain_far, bias_far, left_far, right_far, out,
+    pair, gain, bias, w_left, w_right, weight, left_rows, right_rows, sems,
 ):
     rows, tokens, channels = pair.shape
     pitch = channels + PAD
@@ -28,8 +28,8 @@
         pltpu.make_async_copy(far, near, sems.at[place])
         for place, (far, near) in enumerate(
             zip(
-                (gain_far, bias_far, left_far, right_far, gate_far),
-                (gain, bias, w_left, w_right, w_gate),
+                (gain_far, bias_far, left_far, right_far),
+                (gain, bias, w_left, w_right),
             )
         )
     ]
@@ -39,7 +39,7 @@
         pltpu.make_async_copy(
             pair_far.at[pl.ds(start, stop - start)],
             pair.at[pl.ds(start, stop - start)],
-            sems.at[5 + step],
+            sems.at[4 + step],
         )
         for step, (start, stop) in enumerate(steps)
     ]
@@ -51,7 +51,6 @@
         copy.wait()
     weight[: 2 * channels] = w_left[...].T * 0.5
     weight[2 * channels :] = w_right[...].T * 0.5
-    w_gate[...] = w_gate[...] * 0.5
 
     gains = jnp.broadcast_to(gain[...], (BATCH * tokens, channels)).T
     biases = jnp.broadcast_to(bias[...], (BATCH * tokens, channels)).T
@@ -65,10 +64,6 @@
             spread = jnp.sum(values * values, axis=0, keepdims=True) * (1.0 / channels)
             normed = (values * lax.rsqrt(spread + EPS) * gains + biases).astype(BF16)
             projected = jnp.dot(weight[...], normed, preferred_element_type=F32)
-            gates = lax.dot_general(
-                normed, w_gate[...], (((0,), (0,)), ((), ())), preferred_element_type=F32
-            )
-            gating[pl.ds(row, BATCH)] = 0.5 * jnp.tanh(gates).reshape(BATCH, tokens, channels) + 0.5
             gate_left, left, gate_right, right = jnp.split(projected, 4, axis=0)
             lefts = (jnp.tanh(gate_left) + 1.0) * left
             rights = (jnp.tanh(gate_right) + 1.0) * right
@@ -83,40 +78,67 @@
             out[channel, 1, start:stop, :] = right_rows[place, :].astype(BF16)
 
 
-def edges(pair, gain, bias, w_left, w_right, w_gate):
+def edges(pair, gain, bias, w_left, w_right):
     rows, tokens, channels = pair.shape
     far = pl.BlockSpec(memory_space=pltpu.HBM)
     return pl.pallas_call(
         edges_kernel,
-        in_specs=[far] * 6,
-        out_specs=[pl.BlockSpec(memory_space=pltpu.VMEM)] * 2,
-        out_shape=[
-            jax.ShapeDtypeStruct((channels, 2, rows, tokens), BF16),
-            jax.ShapeDtypeStruct(pair.shape, F32),
-        ],
+        in_specs=[far] * 5,
+        out_specs=pl.BlockSpec(memory_space=pltpu.VMEM),
+        out_shape=jax.ShapeDtypeStruct((channels, 2, rows, tokens), BF16),
         scratch_shapes=[
             pltpu.VMEM(pair.shape, F32),
             pltpu.VMEM(gain.shape, F32),
             pltpu.VMEM(bias.shape, F32),
             pltpu.VMEM(w_left.shape, BF16),
             pltpu.VMEM(w_right.shape, BF16),
-            pltpu.VMEM(w_gate.shape, BF16),
             pltpu.VMEM((4 * channels, channels), BF16),
             pltpu.VMEM((rows * (channels + PAD), tokens), F32),
             pltpu.VMEM((rows * (channels + PAD), tokens), F32),
-            pltpu.SemaphoreType.DMA((7,)),
+            pltpu.SemaphoreType.DMA((6,)),
         ],
         compiler_params=pltpu.CompilerParams(vmem_limit_bytes=28 * 2**20),
         cost_estimate=pl.CostEstimate(
-            flops=10 * rows * tokens * channels * channels,
-            bytes_accessed=12 * rows * tokens * channels,
-            transcendentals=3 * rows * tokens * channels,
+            flops=8 * rows * tokens * channels * channels,
+            bytes_accessed=8 * rows * tokens * channels,
+            transcendentals=2 * rows * tokens * channels,
         ),
         name="edges",
-    )(*in_hbm(pair, gain, bias, w_left, w_right, w_gate))
-
-
-def product_kernel(both, out, left_turned):
+    )(*in_hbm(pair, gain, bias, w_left, w_right))
+
+
+def gating_kernel(pair, gain, bias, weight, gating):
+    rows, tokens, channels = pair.shape
+    values = pair[...].reshape(rows * tokens, channels)
+    center = jnp.mean(values, axis=-1, keepdims=True)
+    values = values - center
+    spread = jnp.mean(values * values, axis=-1, keepdims=True)
+    normed = (values * lax.rsqrt(spread + EPS) * gain[...] + bias[...]).astype(BF16)
+    projected = jnp.dot(normed, weight[...], preferred_element_type=F32)
+    gating[...] = (0.5 * jnp.tanh(0.5 * projected) + 0.5).reshape(rows, tokens, channels)
+
+
+def gates(pair, gain, bias, weight):
+    rows, tokens, channels = pair.shape
+    whole = lambda *shape: pl.BlockSpec(shape, lambda step: (0,) * len(shape))
+    block = pl.BlockSpec((ROWS, tokens, channels), lambda step: (step, 0, 0))
+    return pl.pallas_call(
+        gating_kernel,
+        grid=(rows // ROWS,),
+        in_specs=[block, whole(1, channels), whole(1, channels), whole(channels, channels)],
+        out_specs=block,
+        out_shape=pltpu.VMEM(pair.shape, F32),
+        compiler_params=pltpu.CompilerParams(vmem_limit_bytes=16 * 2**20),
+        cost_estimate=pl.CostEstimate(
+            flops=2 * rows * tokens * channels * channels,
+            bytes_accessed=8 * rows * tokens * channels,
+            transcendentals=rows * tokens * channels,
+        ),
+        name="gates",
+    )(pair, gain, bias, weight)
+
+
+def product_kernel(both, out_far, left_turned, out, sems):
     n_rows, n_cols, _, depth, tokens = both.shape
 
     def column(col, side):
@@ -124,12 +146,20 @@
 
     for col in range(n_cols):
         left_turned[col * tokens : (col + 1) * tokens, :] = column(col, 0).T
+    copies = []
     for col in range(0, n_cols, 2):
         rights = jnp.concatenate([column(col, 1), column(col + 1, 1)], axis=1)
         total = jnp.dot(left_turned[...], rights, preferred_element_type=F32).astype(BF16)
         for part in range(2):
             block = total[:, part * tokens : (part + 1) * tokens]
             out[:, col + part] = block.reshape(n_rows, depth, tokens)
+        place = pl.ds(col, 2)
+        copies.append(
+            pltpu.make_async_copy(out.at[:, place], out_far.at[:, place], sems.at[col // 2])
+        )
+        copies[-1].start()
+    for copy in copies:
+        copy.wait()
 
 
 def products(both):
@@ -137,8 +167,14 @@
     size = n_rows * depth
     return pl.pallas_call(
         product_kernel,
-        out_shape=jax.ShapeDtypeStruct((n_rows, n_cols, depth, tokens), BF16),
-        scratch_shapes=[pltpu.VMEM((size, size), BF16)],
+        in_specs=[pl.BlockSpec(memory_space=pltpu.VMEM)],
+        out_specs=pl.BlockSpec(memory_space=pltpu.HBM),
+        out_shape=pltpu.HBM((n_rows, n_cols, depth, tokens), BF16),
+        scratch_shapes=[
+            pltpu.VMEM((size, size), BF16),
+            pltpu.VMEM((n_rows, n_cols, depth, tokens), BF16),
+            pltpu.SemaphoreType.DMA((n_cols // 2,)),
+        ],
         compiler_params=pltpu.CompilerParams(vmem_limit_bytes=24 * 2**20),
         cost_estimate=pl.CostEstimate(
             flops=2 * size**3, bytes_accessed=6 * size * size, transcendentals=0
@@ -213,7 +249,8 @@
     rows, tokens, channels = pair.shape
     axes = ("row", "col")
     gain, bias = ln_gain[None], ln_bias[None]
-    both, gating = edges(pair, gain, bias, w_left, w_right, w_gate)
+    both = edges(pair, gain, bias, w_left, w_right)
+    gating = gates(pair, gain, bias, w_gate)
     both = lax.all_to_all(both.reshape(channels, 2 * rows, tokens), axes, 0, 0, tiled=True)
     product = products(both.reshape(n_rows, n_cols, 2, rows, tokens)).reshape(channels, rows, tokens)
     product = lax.all_to_all(product, axes, 0, 0, tiled=True)

time: 109 us -> 113 us (1.037)
  blocking collectives: 97.9 us -> 63.1 us
  waiting for transfers between devices: 0 us -> 21.9 us
  local copies, waits for them, and re-layouts: 0.01 us -> 6.39 us
  starting transfers between devices: 0 us -> 5.53 us
  Pallas kernels: 11.3 us -> 15.2 us
    all_to_all x1 -> x0, blocking collectives: 34.8 us -> none  [per_device(): product = lax.all_to_all(product, axes, 0, 0, tiled=True)]
    all_to_all x0 -> x1, waiting for transfers between devices: none -> 21.9 us  [per_device(): product = lax.all_to_all(product, axes, 0, 0, tiled=True)]
    unnamed x6 -> x18, local copies, waits for them, and re-layouts: 0.01 us -> 6.39 us
    all_to_all x0 -> x1, starting transfers between devices: none -> 5.53 us  [per_device(): product = lax.all_to_all(product, axes, 0, 0, tiled=True)]
    pallas_call x2 -> x3, Pallas kernels: 7.95 us -> 11.9 us  [the longest x1 5.15 us: edges(): pl.pallas_call(edges_kernel, in_specs=[far] * 5, out_specs=pl.BlockSpec(m...]
  transfers between devices with their start and end apart: 0 -> 1, of which waited for: 0 -> 1; matrix products, arithmetic and copies ran while one was open for 0% -> 0% of each run, Pallas kernels for 0% -> 3%
where the time goes in v10:
time: 113 us; the launch traced here: 112 us
  blocking collectives  63.1 us (56%)
  waiting for transfers between devices  21.9 us (19%)
  Pallas kernels  15.2 us (13%)
  local copies, waits for them, and re-layouts  6.39 us (6%)
  starting transfers between devices  5.53 us (5%)
    all_to_all x1, blocking collectives, per_device(): lax.all_to_all(both.reshape(channels, 2 * rows, tokens), axes, 0, 0, tile...  63.1 us
    all_to_all x1, waiting for transfers between devices, per_device(): product = lax.all_to_all(product, axes, 0, 0, tiled=True)  21.9 us
    unnamed x18, local copies, waits for them, and re-layouts  6.39 us
    all_to_all x1, starting transfers between devices, per_device(): product = lax.all_to_all(product, axes, 0, 0, tiled=True)  5.53 us
    pallas_call x1, Pallas kernels, edges(): pl.pallas_call(edges_kernel, in_specs=[far] * 5, out_specs=pl.BlockSpec(m...  5.15 us
    pallas_call x1, Pallas kernels, products(): pl.pallas_call(product_kernel, in_specs=[pl.BlockSpec(memory_space=pltpu....  3.46 us
    pallas_call x1, Pallas kernels, update(): pl.pallas_call(update_kernel, in_specs=[pl.BlockSpec(memory_space=pltpu.V...  3.37 us
    pallas_call x1, Pallas kernels, gates(): pl.pallas_call(gating_kernel, grid=(rows // ROWS,), in_specs=[block, whol...  3.25 us
  transfers between devices with their start and end apart: 1, of which 1 were waited for; matrix products, arithmetic and copies ran while one was open for 0% of the time, Pallas kernels for 3%

profile of v10, /device:TPU:0, one launch (start us, length us, event | category | flops | bytes accessed | tf_op | source)
XLA Modules:
  0.0 112.3 jit_solution(10891668578276409408)
XLA Ops:
  0.0 5.2 %edges.1 = bf16[128,2,64,128]{3,2,1,0:T(8,128)(2,1)S(1)} custom-call(f32[64,128,128]{2,1,0:T(8,128)} %pair.1, f32[1,128]{1,0:T(1,128)} %bitcast.9, f32[1,128]{1,0:T(1,128)} %bitcast.11, bf16[128,256]{1,0:T(8,128)(2,1)} %left_far.1, bf16[128,256]{1,0:T(8,128)(2,1)} %right_far.1), custom_call_target="tpu_custom_call" | custom-call | flops 1073741824 | bytes 8388608 | tf_op jit(solution)/shard_map/edges/pallas_call | solution.py:84
  5.2 63.1 %all_to_all.10 = bf16[128,128,128]{2,1,0:T(8,128)(2,1)S(1)} all-to-all(bf16[128,128,128]{2,1,0:T(8,128)(2,1)S(1)} %bitcast.7), channel_id=1, replica_groups=mesh['row'=16,'col'=8] {'row','col'}, dimensions={0} | all-to-all | bytes 8388608 | tf_op jit(solution)/shard_map/all_to_all | solution.py:254
  68.3 0.0 copy-start.3
  68.3 0.0 copy-start.5
  68.3 0.0 copy-start.6
  68.3 3.5 %products.1 = bf16[16,8,64,128]{3,2,1,0:T(8,128)(2,1)} custom-call(bf16[16,8,2,64,128]{4,3,2,1,0:T(8,128)(2,1)S(1)} %bitcast.8), custom_call_target="tpu_custom_call" | custom-call | flops 2147483648 | bytes 6291456 | tf_op jit(solution)/shard_map/products/pallas_call | solution.py:168
  71.7 5.5 %all-to-all-start.1 = ((bf16[128,64,128]{2,1,0:T(8,128)(2,1)}), bf16[128,64,128]{2,1,0:T(8,128)(2,1)S(1)}, u32[]{:S(2)}, u32[]{:S(2)}) async-start(bf16[128,64,128]{2,1,0:T(8,128)(2,1)} %bitcast.15), calls=%async_computation.1 | async-start | bytes 4194304 | tf_op jit(solution)/shard_map/all_to_all | solution.py:256
  77.3 0.0 copy-done.3
  77.3 0.0 copy-done.5
  77.3 0.0 copy-done.6
  77.3 0.0 copy-start
  77.3 2.2 %copy-done = f32[64,128,128]{2,1,0:T(8,128)S(1)} copy-done((f32[64,128,128]{2,1,0:T(8,128)S(1)}, f32[64,128,128]{2,1,0:T(8,128)}, u32[]{:S(2)}) %copy-start) | copy-done | bytes 4194328
  79.5 0.0 copy-start.4
  79.5 0.0 copy-start.7
  79.5 0.0 copy-start.8
  79.5 3.2 %gates.1.gating = f32[64,128,128]{2,1,0:T(8,128)S(1)} custom-call(f32[64,128,128]{2,1,0:T(8,128)S(1)} %copy-done, f32[1,128]{1,0:T(1,128)S(1)} %bitcast.10, f32[1,128]{1,0:T(1,128)S(1)} %bitcast.12, bf16[128,128]{1,0:T(8,128)(2,1)S(1)} %copy-done.3), custom_call_target="tpu_custom_call" | custom-call | flops 268435456 | bytes 8388608 | tf_op jit(solution)/shard_map/gates/pallas_call | solution.py:125
  82.7 0.0 copy-start.1
  82.8 2.0 %copy-done.1 = f32[64,128,128]{2,1,0:T(8,128)} copy-done((f32[64,128,128]{2,1,0:T(8,128)}, f32[64,128,128]{2,1,0:T(8,128)S(1)}, u32[]{:S(2)}) %copy-start.1) | copy-done | bytes 4194328
  84.8 21.9 %all-to-all-done.1.product = bf16[128,64,128]{2,1,0:T(8,128)(2,1)S(1)} async-done(((bf16[128,64,128]{2,1,0:T(8,128)(2,1)}), bf16[128,64,128]{2,1,0:T(8,128)(2,1)S(1)}, u32[]{:S(2)}, u32[]{:S(2)}) %all-to-all-start.1) | async-done | bytes 2097184 | tf_op jit(solution)/shard_map/all_to_all | solution.py:256
  106.7 0.0 copy-done.4
  106.7 0.0 copy-done.7
  106.7 0.0 copy-done.8
  106.7 0.0 copy-start.2
  106.7 2.2 %copy-done.2 = f32[64,128,128]{2,1,0:T(8,128)S(1)} copy-done((f32[64,128,128]{2,1,0:T(8,128)S(1)}, f32[64,128,128]{2,1,0:T(8,128)}, u32[]{:S(2)}) %copy-start.2) | copy-done | bytes 4194328
  108.9 3.4 %update.1 = f32[64,128,128]{2,1,0:T(8,128)} custom-call(bf16[128,64,128]{2,1,0:T(8,128)(2,1)S(1)} %all-to-all-done.1.product, f32[64,128,128]{2,1,0:T(8,128)S(1)} %copy-done.2, f32[1,128]{1,0:T(1,128)S(1)} %bitcast.13, f32[1,128]{1,0:T(1,128)S(1)} %bitcast.14, bf16[128,128]{1,0:T(8,128)(2,1)S(1)} %copy-done.4), custom_call_target="tpu_custom_call" | custom-call | flops 268435456 | bytes 10485760 | tf_op jit(solution)/shard_map/update/pallas_call | solution.py:226
Async XLA Ops:
  68.3 9.0 %copy-start.3 = (bf16[128,128]{1,0:T(8,128)(2,1)S(1)}, bf16[128,128]{1,0:T(8,128)(2,1)}, u32[]{:S(2)}) copy-start(bf16[128,128]{1,0:T(8,128)(2,1)} %weight.2) | copy-start | bytes 98308
  68.3 9.0 %copy-start.5 = (f32[128]{0:T(128)S(1)}, f32[128]{0:T(128)}, u32[]{:S(2)}) copy-start(f32[128]{0:T(128)} %param.10) | copy-start | bytes 1540
  68.3 9.0 %copy-start.6 = (f32[128]{0:T(128)S(1)}, f32[128]{0:T(128)}, u32[]{:S(2)}) copy-start(f32[128]{0:T(128)} %param.11) | copy-start | bytes 1540
  71.7 35.0 %all-to-all-start.1 = ((bf16[128,64,128]{2,1,0:T(8,128)(2,1)}), bf16[128,64,128]{2,1,0:T(8,128)(2,1)S(1)}, u32[]{:S(2)}, u32[]{:S(2)}) async-start(bf16[128,64,128]{2,1,0:T(8,128)(2,1)} %bitcast.15), calls=%async_computation.1 | async-start | bytes 4194304 | tf_op jit(solution)/shard_map/all_to_all | solution.py:256
  77.3 2.2 %copy-start = (f32[64,128,128]{2,1,0:T(8,128)S(1)}, f32[64,128,128]{2,1,0:T(8,128)}, u32[]{:S(2)}) copy-start(f32[64,128,128]{2,1,0:T(8,128)} %pair.1) | copy-start | bytes 12582916
  79.5 27.2 %copy-start.4 = (bf16[128,128]{1,0:T(8,128)(2,1)S(1)}, bf16[128,128]{1,0:T(8,128)(2,1)}, u32[]{:S(2)}) copy-start(bf16[128,128]{1,0:T(8,128)(2,1)} %weight.3) | copy-start | bytes 98308
  79.5 27.2 %copy-start.7 = (f32[128]{0:T(128)S(1)}, f32[128]{0:T(128)}, u32[]{:S(2)}) copy-start(f32[128]{0:T(128)} %param.16) | copy-start | bytes 1540
  79.5 27.2 %copy-start.8 = (f32[128]{0:T(128)S(1)}, f32[128]{0:T(128)}, u32[]{:S(2)}) copy-start(f32[128]{0:T(128)} %param.17) | copy-start | bytes 1540
  82.7 2.0 %copy-start.1 = (f32[64,128,128]{2,1,0:T(8,128)}, f32[64,128,128]{2,1,0:T(8,128)S(1)}, u32[]{:S(2)}) copy-start(f32[64,128,128]{2,1,0:T(8,128)S(1)} %gates.1.gating) | copy-start | bytes 12582916
  106.7 2.2 %copy-start.2 = (f32[64,128,128]{2,1,0:T(8,128)S(1)}, f32[64,128,128]{2,1,0:T(8,128)}, u32[]{:S(2)}) copy-start(f32[64,128,128]{2,1,0:T(8,128)} %copy-done.1) | copy-start | bytes 12582916

commit v11 on v9

--- a/solution.py
+++ b/solution.py
@@ -47,17 +47,21 @@
     for copy in small:
         copy.start()
     fetches[1].start()
-    for copy in small:
+    for copy in small[:2]:
+        copy.wait()
+    gains = jnp.broadcast_to(gain[...], (BATCH * tokens, channels)).T
+    biases = jnp.broadcast_to(bias[...], (BATCH * tokens, channels)).T
+
+    fetches[0].wait()
+    for copy in small[2:]:
         copy.wait()
     weight[: 2 * channels] = w_left[...].T * 0.5
     weight[2 * channels :] = w_right[...].T * 0.5
     w_gate[...] = w_gate[...] * 0.5
 
-    gains = jnp.broadcast_to(gain[...], (BATCH * tokens, channels)).T
-    biases = jnp.broadcast_to(bias[...], (BATCH * tokens, channels)).T
-
     for copy, (start, stop) in zip(fetches, steps):
-        copy.wait()
+        if start > 0:
+            copy.wait()
         for row in range(start, stop, BATCH):
             values = pair[pl.ds(row, BATCH)].reshape(BATCH * tokens, channels).T
             center = jnp.sum(values, axis=0, keepdims=True) * (1.0 / channels)

time: 109 us -> 109 us (level)
  no operation moved by 1% of the time
where the time goes in v11:
time: 109 us
  blocking collectives  97.9 us (90%)
  Pallas kernels  11.2 us (10%)
    all_to_all x1, blocking collectives, per_device(): lax.all_to_all(both.reshape(channels, 2 * rows, tokens), axes, 0, 0, tile...  63.1 us
    all_to_all x1, blocking collectives, per_device(): product = lax.all_to_all(product, axes, 0, 0, tiled=True)  34.8 us
    pallas_call x1, Pallas kernels, edges(): pl.pallas_call(edges_kernel, in_specs=[far] * 6, out_specs=[pl.BlockSpec(...  5.45 us
    pallas_call x1, Pallas kernels, update(): pl.pallas_call(update_kernel, in_specs=[pl.BlockSpec(memory_space=pltpu.V...  3.36 us
    pallas_call x1, Pallas kernels, products(): pl.pallas_call(product_kernel, out_shape=jax.ShapeDtypeStruct((n_rows, n_...  2.36 us

profile of v11, /device:TPU:0, one launch (start us, length us, event | category | flops | bytes accessed | tf_op | source)
XLA Modules:
  0.0 109.1 jit_solution(15068695663507853193)
XLA Ops:
  0.0 5.4 %edges.1 = (bf16[128,2,64,128]{3,2,1,0:T(8,128)(2,1)S(1)}, f32[64,128,128]{2,1,0:T(8,128)S(1)}) custom-call(f32[64,128,128]{2,1,0:T(8,128)} %pair_far.1, f32[1,128]{1,0:T(1,128)} %bitcast.12, f32[1,128]{1,0:T(1,128)} %bitcast.13, bf16[128,256]{1,0:T(8,128)(2,1)} %left_far.1, bf16[128,256]{1,0:T(8,128)(2,1)} %right_far.1, bf16[128,128]{1,0:T(8,128)(2,1)} %gate_far.1), custom_call_target="tpu_custom_call" | custom-call | flops 1342177280 | bytes 12582912 | tf_op jit(solution)/shard_map/edges/pallas_call | solution.py:93
  5.5 63.1 %all_to_all.10 = bf16[128,128,128]{2,1,0:T(8,128)(2,1)S(1)} all-to-all(bf16[128,128,128]{2,1,0:T(8,128)(2,1)S(1)} %bitcast.7), channel_id=1, replica_groups=mesh['row'=16,'col'=8] {'row','col'}, dimensions={0} | all-to-all | bytes 8388608 | tf_op jit(solution)/shard_map/all_to_all | solution.py:221
  68.6 0.0 copy-start
  68.6 0.0 copy-start.1
  68.6 0.0 copy-start.2
  68.6 2.4 %products.1 = bf16[16,8,64,128]{3,2,1,0:T(8,128)(2,1)S(1)} custom-call(bf16[16,8,2,64,128]{4,3,2,1,0:T(8,128)(2,1)S(1)} %bitcast.8), custom_call_target="tpu_custom_call" | custom-call | flops 2147483648 | bytes 6291456 | tf_op jit(solution)/shard_map/products/pallas_call | solution.py:142
  70.9 34.8 %all_to_all.11.product = bf16[128,64,128]{2,1,0:T(8,128)(2,1)S(1)} all-to-all(bf16[128,64,128]{2,1,0:T(8,128)(2,1)S(1)} %bitcast.9), channel_id=1, replica_groups=mesh['row'=16,'col'=8] {'row','col'}, dimensions={0} | all-to-all | bytes 4194304 | tf_op jit(solution)/shard_map/all_to_all | solution.py:223
  105.7 0.0 copy-done
  105.7 0.0 copy-done.1
  105.7 0.0 copy-done.2
  105.7 3.4 %update.1 = f32[64,128,128]{2,1,0:T(8,128)} custom-call(bf16[128,64,128]{2,1,0:T(8,128)(2,1)S(1)} %all_to_all.11.product, f32[64,128,128]{2,1,0:T(8,128)S(1)} %get-tuple-element.8.gating, f32[1,128]{1,0:T(1,128)S(1)} %bitcast.10, f32[1,128]{1,0:T(1,128)S(1)} %bitcast.11, bf16[128,128]{1,0:T(8,128)(2,1)S(1)} %copy-done), custom_call_target="tpu_custom_call" | custom-call | flops 268435456 | bytes 10485760 | tf_op jit(solution)/shard_map/update/pallas_call | solution.py:194
Async XLA Ops:
  68.6 37.1 %copy-start = (bf16[128,128]{1,0:T(8,128)(2,1)S(1)}, bf16[128,128]{1,0:T(8,128)(2,1)}, u32[]{:S(2)}) copy-start(bf16[128,128]{1,0:T(8,128)(2,1)} %weight.1) | copy-start | bytes 98308
  68.6 37.1 %copy-start.1 = (f32[128]{0:T(128)S(1)}, f32[128]{0:T(128)}, u32[]{:S(2)}) copy-start(f32[128]{0:T(128)} %param.16) | copy-start | bytes 1540
  68.6 37.1 %copy-start.2 = (f32[128]{0:T(128)S(1)}, f32[128]{0:T(128)}, u32[]{:S(2)}) copy-start(f32[128]{0:T(128)} %param.17) | copy-start | bytes 1540

commit v12 on v11

--- a/solution.py
+++ b/solution.py
@@ -43,8 +43,10 @@
         )
         for step, (start, stop) in enumerate(steps)
     ]
+    for copy in small[:2]:
+        copy.start()
     fetches[0].start()
-    for copy in small:
+    for copy in small[2:]:
         copy.start()
     fetches[1].start()
     for copy in small[:2]:

time: 109 us -> 109 us (level)
  no operation moved by 1% of the time
where the time goes in v12:
time: 109 us
  blocking collectives  97.9 us (90%)
  Pallas kernels  11.2 us (10%)
    all_to_all x1, blocking collectives, per_device(): lax.all_to_all(both.reshape(channels, 2 * rows, tokens), axes, 0, 0, tile...  63.1 us
    all_to_all x1, blocking collectives, per_device(): product = lax.all_to_all(product, axes, 0, 0, tiled=True)  34.8 us
    pallas_call x1, Pallas kernels, edges(): pl.pallas_call(edges_kernel, in_specs=[far] * 6, out_specs=[pl.BlockSpec(...  5.48 us
    pallas_call x1, Pallas kernels, update(): pl.pallas_call(update_kernel, in_specs=[pl.BlockSpec(memory_space=pltpu.V...  3.36 us
    pallas_call x1, Pallas kernels, products(): pl.pallas_call(product_kernel, out_shape=jax.ShapeDtypeStruct((n_rows, n_...  2.36 us

profile of v12, /device:TPU:0, one launch (start us, length us, event | category | flops | bytes accessed | tf_op | source)
XLA Modules:
  0.0 109.1 jit_solution(14690472508072250635)
XLA Ops:
  0.0 5.5 %edges.1 = (bf16[128,2,64,128]{3,2,1,0:T(8,128)(2,1)S(1)}, f32[64,128,128]{2,1,0:T(8,128)S(1)}) custom-call(f32[64,128,128]{2,1,0:T(8,128)} %pair_far.1, f32[1,128]{1,0:T(1,128)} %bitcast.12, f32[1,128]{1,0:T(1,128)} %bitcast.13, bf16[128,256]{1,0:T(8,128)(2,1)} %left_far.1, bf16[128,256]{1,0:T(8,128)(2,1)} %right_far.1, bf16[128,128]{1,0:T(8,128)(2,1)} %gate_far.1), custom_call_target="tpu_custom_call" | custom-call | flops 1342177280 | bytes 12582912 | tf_op jit(solution)/shard_map/edges/pallas_call | solution.py:95
  5.5 63.1 %all_to_all.10 = bf16[128,128,128]{2,1,0:T(8,128)(2,1)S(1)} all-to-all(bf16[128,128,128]{2,1,0:T(8,128)(2,1)S(1)} %bitcast.7), channel_id=1, replica_groups=mesh['row'=16,'col'=8] {'row','col'}, dimensions={0} | all-to-all | bytes 8388608 | tf_op jit(solution)/shard_map/all_to_all | solution.py:223
  68.6 0.0 copy-start
  68.6 0.0 copy-start.1
  68.6 0.0 copy-start.2
  68.6 2.4 %products.1 = bf16[16,8,64,128]{3,2,1,0:T(8,128)(2,1)S(1)} custom-call(bf16[16,8,2,64,128]{4,3,2,1,0:T(8,128)(2,1)S(1)} %bitcast.8), custom_call_target="tpu_custom_call" | custom-call | flops 2147483648 | bytes 6291456 | tf_op jit(solution)/shard_map/products/pallas_call | solution.py:144
  71.0 34.8 %all_to_all.11.product = bf16[128,64,128]{2,1,0:T(8,128)(2,1)S(1)} all-to-all(bf16[128,64,128]{2,1,0:T(8,128)(2,1)S(1)} %bitcast.9), channel_id=1, replica_groups=mesh['row'=16,'col'=8] {'row','col'}, dimensions={0} | all-to-all | bytes 4194304 | tf_op jit(solution)/shard_map/all_to_all | solution.py:225
  105.7 0.0 copy-done
  105.7 0.0 copy-done.1
  105.7 0.0 copy-done.2
  105.7 3.4 %update.1 = f32[64,128,128]{2,1,0:T(8,128)} custom-call(bf16[128,64,128]{2,1,0:T(8,128)(2,1)S(1)} %all_to_all.11.product, f32[64,128,128]{2,1,0:T(8,128)S(1)} %get-tuple-element.8.gating, f32[1,128]{1,0:T(1,128)S(1)} %bitcast.10, f32[1,128]{1,0:T(1,128)S(1)} %bitcast.11, bf16[128,128]{1,0:T(8,128)(2,1)S(1)} %copy-done), custom_call_target="tpu_custom_call" | custom-call | flops 268435456 | bytes 10485760 | tf_op jit(solution)/shard_map/update/pallas_call | solution.py:196
Async XLA Ops:
  68.6 37.1 %copy-start = (bf16[128,128]{1,0:T(8,128)(2,1)S(1)}, bf16[128,128]{1,0:T(8,128)(2,1)}, u32[]{:S(2)}) copy-start(bf16[128,128]{1,0:T(8,128)(2,1)} %weight.1) | copy-start | bytes 98308
  68.6 37.1 %copy-start.1 = (f32[128]{0:T(128)S(1)}, f32[128]{0:T(128)}, u32[]{:S(2)}) copy-start(f32[128]{0:T(128)} %param.16) | copy-start | bytes 1540
  68.6 37.1 %copy-start.2 = (f32[128]{0:T(128)S(1)}, f32[128]{0:T(128)}, u32[]{:S(2)}) copy-start(f32[128]{0:T(128)} %param.17) | copy-start | bytes 1540
